TPU v7x, 256 devices: a whole 4x4x8 slice. The times are simulated.
256 devices in a mesh: dp: 16 (over z_lo, y, core), seq: 16 (over z_hi, x).
Axes of the slice: x: 4, y: 4, z: 8 (z_hi: 4, z_lo: 2; z = z_hi * 2 + z_lo), core: 2. Of those that a mesh axis runs over, the one named last changes fastest.
Arguments:
- inputs: bfloat16 [16, 2048, 6144], P('dp', 'seq'), may hold values from -6 to 6
- queries: bfloat16 [16, 2048, 3072], P('dp', 'seq'), may hold values from -12 to 12
- values: bfloat16 [16, 2048, 512], P('dp', 'seq'), may hold values from -6 to 6
- key_weight: bfloat16 [6144, 512], P('seq'), may hold values from -0.078125 to 0.078125
- doc_ids: int32 [16, 2048], P('dp'), may hold values from 0 to 7, never falling along the last dimension, each value on 1 to 1024 neighbouring positions
- grad_out: bfloat16 [16, 2048, 3072], P('dp', 'seq'), may hold values from -24 to 24
Outputs:
- attn_out: bfloat16 [16, 2048, 3072], P('dp', 'seq')
- grad_queries: bfloat16 [16, 2048, 3072], P('dp', 'seq')
- grad_values: bfloat16 [16, 2048, 512], P('dp', 'seq')
- grad_key_weight: float32 [6144, 512], P('seq')
Inputs may be any that keep to these rules, and one draw needn't show every extreme that they name: `doc_ids`: along each window the document number never falls; each document holds 1 to 1024 tokens and one holds exactly 1024.
All inputs are finite; a program needn't handle non-finite values.
Results may differ from a plain program's by a relative error of at most 0.02.
Values may be sent and summed in bfloat16 or wider, within the bound.
A program may use at most 128 MiB of HBM per device.

v0:
```python
import math

import jax
import jax.numpy as jnp
from jax import lax
from jax.sharding import PartitionSpec as P

QH = 24
KVH = 4
HD = 128


ROPE_BASE = 1000000.0


def rotate(field, position, heads, sign):
    count = field.shape[0]
    width = field.shape[1] // heads
    half = width // 2
    shaped = field.reshape(count, heads, width)
    freqs = ROPE_BASE ** (-(jnp.arange(half).astype(jnp.float32) * 2.0 / width))
    angles = position.astype(jnp.float32)[:, None] * freqs[None, :]
    cosine = jnp.cos(angles)[:, None, :]
    sine = jnp.sin(angles)[:, None, :]
    first = shaped[..., :half]
    second = shaped[..., half:]
    out_first = first * cosine - sign * second * sine
    out_second = sign * first * sine + second * cosine
    return jnp.concatenate([out_first, out_second], axis=-1).reshape(count, heads * width)


def local(inputs, queries, values, key_weight, doc_ids, grad_out):
    hidden = inputs[0]
    query_rows = queries[0]
    value_rows = values[0]
    cot_rows = grad_out[0]
    docs = doc_ids[0]
    tok_rows = hidden.shape[0]
    kv_width = value_rows.shape[1]
    q_width = query_rows.shape[1]
    group = QH // KVH
    scale = 1.0 / math.sqrt(HD)
    whole = tok_rows * lax.axis_size("seq")
    offset = lax.axis_index("seq") * tok_rows
    positions = offset + jnp.arange(tok_rows)
    query_docs = lax.dynamic_slice_in_dim(docs, offset, tok_rows, 0)
    key_raw = jnp.dot(
        hidden,
        lax.all_gather(key_weight, "seq", axis=0, tiled=True),
        preferred_element_type=jnp.float32,
    )
    keys = rotate(key_raw, positions, KVH, 1.0).astype(jnp.bfloat16)
    key_all, value_all = (
        lax.all_gather(keys, "seq", axis=0, tiled=True),
        lax.all_gather(value_rows, "seq", axis=0, tiled=True),
    )
    tile = math.gcd(whole, 512)
    count = whole // tile
    key_tiles = key_all.reshape(count, tile, KVH, HD)
    value_tiles = value_all.reshape(count, tile, KVH, HD)
    doc_tiles = docs.reshape(count, tile)
    anchors = jnp.arange(count) * tile
    query_heads = query_rows.reshape(tok_rows, KVH, group, HD)
    cot_heads = cot_rows.reshape(tok_rows, KVH, group, HD)

    def visible(doc_tile, anchor):
        key_pos = anchor + jnp.arange(tile)
        return (query_docs[:, None] == doc_tile[None, :]) & (positions[:, None] >= key_pos[None, :])

    def exp_weights(key_tile, doc_tile, anchor):
        scores = (
            jnp.einsum("tkgd,ckd->kgtc", query_heads, key_tile, preferred_element_type=jnp.float32)
            * scale
        )
        return jnp.where(visible(doc_tile, anchor)[None, None], jnp.exp(scores), 0.0)

    zero_sum = jnp.zeros((KVH, group, tok_rows), jnp.float32)
    zero_mix = jnp.zeros((tok_rows, KVH, group, HD), jnp.float32)

    def forward_tile(key_tile, value_tile, doc_tile, anchor):
        weights = exp_weights(key_tile, doc_tile, anchor)
        mixed = jnp.einsum(
            "kgtc,ckd->tkgd",
            weights.astype(jnp.bfloat16),
            value_tile,
            preferred_element_type=jnp.float32,
        )
        return (jnp.sum(weights, axis=-1), mixed)

    def forward_step(carry, item):
        key_tile, value_tile, doc_tile, anchor = item
        part_sum, part_mix = forward_tile(key_tile, value_tile, doc_tile, anchor)
        return ((carry[0] + part_sum, carry[1] + part_mix), None)

    (sums, mixes), _ = lax.scan(
        forward_step, (zero_sum, zero_mix), (key_tiles, value_tiles, doc_tiles, anchors)
    )
    attended = (mixes / jnp.transpose(sums, (2, 0, 1))[..., None]).astype(jnp.bfloat16)
    delta = jnp.transpose(
        jnp.sum(cot_heads.astype(jnp.float32) * attended.astype(jnp.float32), axis=-1), (1, 2, 0)
    )

    def backward_tile(key_tile, value_tile, doc_tile, anchor):
        probs = exp_weights(key_tile, doc_tile, anchor) / sums[..., None]
        dvalue = jnp.einsum(
            "kgtc,tkgd->ckd",
            probs.astype(jnp.bfloat16),
            cot_heads,
            preferred_element_type=jnp.float32,
        )
        dprobs = jnp.einsum(
            "tkgd,ckd->kgtc", cot_heads, value_tile, preferred_element_type=jnp.float32
        )
        dscores = (probs * (dprobs - delta[..., None])).astype(jnp.bfloat16)
        dquery = (
            jnp.einsum("kgtc,ckd->tkgd", dscores, key_tile, preferred_element_type=jnp.float32)
            * scale
        )
        dkey = (
            jnp.einsum("kgtc,tkgd->ckd", dscores, query_heads, preferred_element_type=jnp.float32)
            * scale
        )
        joined = jnp.concatenate(
            [dkey.reshape(tile, kv_width), dvalue.reshape(tile, kv_width)], axis=1
        )
        return (dquery, joined)

    def backward_step(carry, item):
        key_tile, value_tile, doc_tile, anchor = item
        dquery, joined = backward_tile(key_tile, value_tile, doc_tile, anchor)
        return (carry + dquery, joined)

    dquery_sum, grad_tiles = lax.scan(
        backward_step, zero_mix, (key_tiles, value_tiles, doc_tiles, anchors)
    )
    terms = grad_tiles.reshape(whole, 2 * kv_width)
    mine = lax.psum_scatter(terms, "seq", scatter_dimension=0, tiled=True)
    grad_value_rows = mine[:, kv_width:].astype(jnp.bfloat16)
    key_grad_raw = rotate(mine[:, :kv_width], positions, KVH, -1.0).astype(jnp.bfloat16)
    partial_grad = lax.psum_scatter(
        lax.dot_general(
            hidden, key_grad_raw, (((0,), (0,)), ((), ())), preferred_element_type=jnp.float32
        ),
        "seq",
        scatter_dimension=0,
        tiled=True,
    )
    weight_grad = lax.psum(partial_grad, "dp") / lax.axis_size("dp")
    attn_rows = attended.reshape(tok_rows, q_width)
    grad_query_rows = dquery_sum.astype(jnp.bfloat16).reshape(tok_rows, q_width)
    return (attn_rows[None], grad_query_rows[None], grad_value_rows[None], weight_grad)


def solution(mesh):
    in_specs = (
        P("dp", "seq", None),
        P("dp", "seq", None),
        P("dp", "seq", None),
        P("seq", None),
        P("dp", None),
        P("dp", "seq", None),
    )
    out_specs = (P("dp", "seq", None), P("dp", "seq", None), P("dp", "seq", None), P("seq", None))
    return jax.shard_map(local, mesh=mesh, in_specs=in_specs, out_specs=out_specs, check_vma=False)
```

profile of v0, /device:TPU:9, one launch (start us, length us, event | category | flops | bytes accessed | tf_op | source)
XLA Modules:
  0.0 778.5 jit_solution(9968016652014360841)
XLA Ops:
  9.6 101.0 %all-gather.5.cloned.1.call-done = bf16[6144,512]{1,0:T(8,128)(2,1)} async-done(((bf16[384,512]{1,0:T(8,128)(2,1)}), bf16[6144,512]{1,0:T(8,128)(2,1)}) %all-gather.5.cloned.1.call-update) | async-done | bytes 6291472 | tf_op jit(solution)/shard_map/all_gather | solution.py:49
  110.5 8.7 %copy.34 = bf16[512,6144]{1,0:T(8,128)(2,1)} copy(bf16[512,6144]{0,1:T(8,128)(2,1)} %bitcast.167) | data formatting | bytes 12582912 | tf_op jit(solution)/shard_map/dot_general | solution.py:47
  119.2 4.6 fusion.32
  126.2 2.3 copy.36
  128.4 2.3 copy.38
  130.7 2.3 copy.40
  133.0 37.4 %all-gather.9.cloned.1.call-done = bf16[1,2048,512]{2,1,0:T(8,128)(2,1)} async-done(((bf16[1,128,512]{2,1,0:T(8,128)(2,1)}), bf16[1,2048,512]{2,1,0:T(8,128)(2,1)}) %all-gather.9.cloned.1.call-update) | async-done | bytes 2097168 | tf_op jit(solution)/shard_map/all_gather | solution.py:55
  170.4 4.0 reshape.220
  174.5 56.4 %all-gather.7.cloned.1.call-done = bf16[2048,512]{1,0:T(8,128)(2,1)} async-done(((bf16[128,512]{1,0:T(8,128)(2,1)}), bf16[2048,512]{1,0:T(8,128)(2,1)}) %all-gather.7.cloned.1.call-update) | async-done | bytes 2097168 | tf_op jit(solution)/shard_map/all_gather | solution.py:54
  230.9 4.0 reshape.219
  234.9 3.3 copy.37
  238.2 45.2 %while.26 = (s32[]{:T(128)}, f32[4,6,128]{2,1,0:T(8,128)S(1)}, f32[128,4,6,128]{0,3,2,1:T(8,128)}, s32[128]{0:T(128)S(1)}, s32[4,512]{1,0:T(4,128)S(1)}, /*index...) while((s32[]{:T(128)}, f32[4,6,128]{2,1,0:T(8,128)S(1)}, ...), condition=%wide.region_2.3_spmd.clone, body=%wide.region_0.2_spmd.clone.sunk | while | flops 815730304 | bytes 34598652 | solution.py:95
  239.7 2.0 constant_dynamic-slice_fusion.9
  241.7 2.1 copy.73
  243.9 2.9 fusion.65
  246.8 1.6 bitcast_add_fusion.4
  251.0 2.0 constant_dynamic-slice_fusion.9
  253.0 2.1 copy.73
  255.1 2.9 fusion.65
  258.0 1.6 bitcast_add_fusion.4
  259.6 1.2 copy-done.3
  262.3 2.0 constant_dynamic-slice_fusion.9
  264.3 2.1 copy.73
  266.4 2.9 fusion.65
  269.3 1.6 bitcast_add_fusion.4
  273.6 2.0 constant_dynamic-slice_fusion.9
  275.6 2.1 copy.73
  277.7 2.9 fusion.65
  280.6 1.6 bitcast_add_fusion.4
  283.4 2.9 multiply_reduce_fusion
  286.2 74.7 %while.27 = (s32[]{:T(128)}, f32[128,4,6,128]{0,3,2,1:T(8,128)S(1)}, f32[4,512,1024]{2,1,0:T(8,128)}, bf16[4,512,4,128]{3,1,2,0:T(8,128)(2,1)}, s32[128]{0:T(128...) while((s32[]{:T(128)}, ...), condition=%wide.region_5.6_spmd.clone, body=%wide.region_4.5_spmd.clone.sunk | while | flops 2026439296 | bytes 58363644 | solution.py:133
  287.7 1.2 constant_dynamic-slice_fusion.11
  288.9 2.7 fusion.75
  295.2 2.2 bitcast_add_fusion.5
  297.3 1.5 maximum_bitcast_fusion.2
  298.8 2.9 copy.75
  301.7 3.2 constant_dynamic-update-slice_fusion.2
  306.4 1.2 constant_dynamic-slice_fusion.11
  307.6 2.7 fusion.75
  313.8 2.2 bitcast_add_fusion.5
  316.0 1.5 maximum_bitcast_fusion.2
  317.5 2.9 copy.75
  320.4 3.2 constant_dynamic-update-slice_fusion.2
  325.0 1.2 constant_dynamic-slice_fusion.11
  326.3 2.7 fusion.75
  332.5 2.2 bitcast_add_fusion.5
  334.7 1.5 maximum_bitcast_fusion.2
  336.1 2.9 copy.75
  339.0 3.2 constant_dynamic-update-slice_fusion.2
  343.7 1.2 constant_dynamic-slice_fusion.11
  344.9 2.7 fusion.75
  351.2 2.2 bitcast_add_fusion.5
  353.3 1.5 maximum_bitcast_fusion.2
  354.8 2.9 copy.75
  357.7 3.2 constant_dynamic-update-slice_fusion.2
  361.2 119.1 %reduce-scatter.3.cloned.1.call-done = f32[128,1024]{1,0:T(8,128)} async-done(((f32[2048,1024]{1,0:T(8,128)}), f32[128,1024]{1,0:T(8,128)}) %reduce-scatter.3.cloned.1.call-update) | async-done | bytes 524304 | tf_op jit(solution)/shard_map/reduce_scatter | solution.py:137
  480.3 1.7 slice.28
  483.2 6.3 convolution_bitcast_fusion.1
  489.5 159.0 %reduce-scatter.5.cloned.1.call-done = f32[384,512]{0,1:T(8,128)} async-done(((f32[6144,512]{0,1:T(8,128)}), f32[384,512]{0,1:T(8,128)}) %reduce-scatter.5.cloned.1.call-update) | async-done | bytes 786448 | tf_op jit(solution)/shard_map/reduce_scatter | solution.py:140
  648.6 2.3 copy.45
  651.9 2.3 copy.46
  654.2 1.6 fusion.35
  655.8 113.6 %all-reduce.2.cloned.1.call-done = f32[384,512]{0,1:T(8,128)} async-done(((f32[384,512]{0,1:T(8,128)}), f32[384,512]{0,1:T(8,128)}) %all-reduce.2.cloned.1.call-update) | async-done | bytes 786448 | tf_op jit(solution)/shard_map/psum | solution.py:148
  769.3 1.2 broadcast_multiply_fusion
  (137 shorter events, 37.1 us)
Async XLA Ops:
  7.2 112.1 %copy-start = (bf16[1,128,6144]{2,1,0:T(8,128)(2,1)S(1)}, bf16[1,128,6144]{2,1,0:T(8,128)(2,1)}, u32[]{:S(2)}) copy-start(bf16[1,128,6144]{2,1,0:T(8,128)(2,1)} %param.10) | copy-start | bytes 4718596
  7.2 103.3 %all-gather.5.cloned.1.call-start = ((), (), s32[]{:S(2)}) async-start(), calls=%async_computation.2 | async-start | bytes 6684672 | tf_op jit(solution)/shard_map/all_gather | solution.py:49
  7.9 162.5 %all-gather.9.cloned.1.call-start = ((), (), s32[]{:S(2)}) async-start(), calls=%async_computation.7 | async-start | bytes 2228224 | tf_op jit(solution)/shard_map/all_gather | solution.py:55
  8.7 222.2 %all-gather.7.cloned.1.call-start = ((), (), s32[]{:S(2)}) async-start(), calls=%async_computation.3 | async-start | bytes 2228224 | tf_op jit(solution)/shard_map/all_gather | solution.py:54
  9.5 114.3 %copy-start.6 = (f32[128,64]{0,1:T(8,128)}, f32[128,64]{0,1:T(8,128)S(1)}, u32[]{:S(2)}) copy-start(f32[128,64]{0,1:T(8,128)S(1)} %get-tuple-element.307) | copy-start | bytes 98308
  119.2 6.3 copy-start.9
  124.7 355.6 %reduce-scatter.3.cloned.1.call-start = ((), (), s32[]{:S(2)}) async-start(), calls=%async_computation.4 | async-start | bytes 8912896 | tf_op jit(solution)/shard_map/reduce_scatter | solution.py:137
  243.9 2.9 copy-start.2
  243.9 2.9 copy-start.4
  248.3 1.2 copy-start.3
  255.1 2.9 copy-start.2
  255.1 2.9 copy-start.4
  259.6 1.2 copy-start.3
  266.4 2.9 copy-start.2
  266.4 2.9 copy-start.4
  270.9 1.2 copy-start.3
  277.7 2.9 copy-start.2
  277.7 2.9 copy-start.4
  282.2 1.2 copy-start.3
  288.9 2.8 copy-start.1
  292.8 1.1 copy-start.5
  307.6 2.8 copy-start.1
  311.5 1.1 copy-start.5
  326.3 2.8 copy-start.1
  330.2 1.1 copy-start.5
  344.9 2.8 copy-start.1
  348.8 1.1 copy-start.5
  360.9 122.2 %copy-start.7 = (f32[128,64]{0,1:T(8,128)S(1)}, f32[128,64]{0,1:T(8,128)}, u32[]{:S(2)}) copy-start(f32[128,64]{0,1:T(8,128)} %copy-done.6) | copy-start | bytes 98308
  360.9 122.2 %copy-start.8 = (f32[128,64]{0,1:T(8,128)S(1)}, f32[128,64]{0,1:T(8,128)}, u32[]{:S(2)}) copy-start(f32[128,64]{0,1:T(8,128)} %get-tuple-element.305) | copy-start | bytes 98308
  360.9 287.6 %reduce-scatter.5.cloned.1.call-start = ((), (), s32[]{:S(2)}) async-start(), calls=%async_computation.5 | async-start | bytes 13369344 | tf_op jit(solution)/shard_map/reduce_scatter | solution.py:140
  489.5 279.9 %all-reduce.2.cloned.1.call-start = ((), (), s32[]{:S(2)}) async-start(), calls=%async_computation.6 | async-start | bytes 1572864 | tf_op jit(solution)/shard_map/psum | solution.py:148
Sparse Core Ops, SparseCore 0:
  10.4 100.0 all-gather.4
  112.9 57.4 all-gather.8
  173.5 57.3 all-gather.6
  361.1 119.2 reduce-scatter.2
  489.6 158.8 reduce-scatter.4
  651.0 118.2 all-reduce.1
where the time goes:
time: 785 us; the launch traced here: 779 us
  waiting for transfers between devices  588 us (75%)
  local copies, waits for them, and re-layouts  94.3 us (12%)
  matrix products  61.3 us (8%)
  other arithmetic  19.4 us (2%)
  between operations  14.3 us (2%)
    reduce_scatter x1, waiting for transfers between devices, local(): lax.psum_scatter(lax.dot_general(hidden, key_grad_raw, (((0,), (0,)), (()...  159 us
    reduce_scatter x1, waiting for transfers between devices, local(): mine = lax.psum_scatter(terms, 'seq', scatter_dimension=0, tiled=True)  119 us
    psum x1, waiting for transfers between devices, local(): weight_grad = lax.psum(partial_grad, 'dp') / lax.axis_size('dp')  114 us
    all_gather x1, waiting for transfers between devices, local(): lax.all_gather(key_weight, 'seq', axis=0, tiled=True)  101 us
    all_gather x1, waiting for transfers between devices, local(): lax.all_gather(keys, 'seq', axis=0, tiled=True)  56.4 us
    all_gather x1, waiting for transfers between devices, local(): lax.all_gather(value_rows, 'seq', axis=0, tiled=True)  37.4 us
    dynamic_slice x28, local copies, waits for them, and re-layouts, local(): lax.scan(forward_step, (zero_sum, zero_mix), (key_tiles, value_tiles, doc...  26.4 us
    dynamic_update_slice x8, local copies, waits for them, and re-layouts, local(): lax.scan(backward_step, zero_mix, (key_tiles, value_tiles, doc_tiles, anc...  24.4 us
  transfers between devices with their start and end apart: 6, of which 6 were waited for; matrix products, arithmetic and copies ran while one was open for 4% of the time, Pallas kernels for 0%

commit v1 on v0

v1 whole, which is shorter than its diff:
```python
import math

import jax
import jax.numpy as jnp
from jax import lax
from jax.experimental import pallas as pl
from jax.experimental.pallas import tpu as pltpu
from jax.sharding import PartitionSpec as P

QH = 24
KVH = 4
HD = 128
GROUP = QH // KVH
ROPE_BASE = 1000000.0
MESH = pl.DeviceIdType.MESH
BF = jnp.bfloat16
F32 = jnp.float32
NQ = 4
VMEM_LIMIT = 56 * 1024 * 1024


class Place:
    def __init__(self):
        dp = lax.axis_index("dp")
        sq = lax.axis_index("seq")
        self.lo = dp // 8
        self.y = (dp // 2) % 4
        self.c = dp % 2
        self.zh = sq // 4
        self.x = sq % 4
        self.j = dp % 8

    def at(self, lo=None, y=None, c=None, zh=None, x=None):
        lo = self.lo if lo is None else lo
        y = self.y if y is None else y
        c = self.c if c is None else c
        zh = self.zh if zh is None else zh
        x = self.x if x is None else x
        return (lo * 8 + y * 2 + c, zh * 4 + x)

    def z_next(self):
        return self.at(lo=1 - self.lo, zh=(self.zh + self.lo) % 4)

    def z_prev(self):
        return self.at(lo=1 - self.lo, zh=(self.zh + 3 + self.lo) % 4)


class Copies:
    def __init__(self, send, recv):
        self.send, self.recv, self.count = send, recv, 0

    def new(self, number=1):
        first = self.count
        self.count += number
        return first

    def make(self, src, dst, index, device):
        return pltpu.make_async_remote_copy(
            src_ref=src,
            dst_ref=dst,
            send_sem=self.send.at[index],
            recv_sem=self.recv.at[index],
            device_id=device,
            device_id_type=MESH,
        )


def greet(devices):
    barrier = pltpu.get_barrier_semaphore()
    for device in devices:
        pl.semaphore_signal(barrier, inc=1, device_id=device, device_id_type=MESH)
    pl.semaphore_wait(barrier, len(devices))


def kind(source, reader):
    return jnp.where(reader > source, 0, 2)


class Gather:
    def __init__(self, place, copies, buf):
        self.p, self.copies, self.buf = place, copies, buf
        p = place
        x = p.x
        self.xl, self.xr = (x + 3) % 4, (x + 1) % 4
        self.left, self.right = p.at(x=self.xl), p.at(x=self.xr)
        self.up = p.at(zh=(p.zh + 1) % 4)
        self.kr, self.kl = kind(x, self.xr), kind(x, self.xl)
        self.fr = jnp.where(self.xl < 2, kind(self.xl, self.xr), 1)
        self.fl = jnp.where(self.xr < 2, 1, kind(self.xr, self.xl))
        self.base = copies.new(16)
        self.sent = []

    def cp(self, what, h, xs, k, device):
        at = pl.ds(256 * h, 256)
        to = k + 1 if what < 2 else k
        return self.copies.make(
            self.buf.at[xs, k, :, at], self.buf.at[xs, to, :, at], self.base + 2 * what + h, device
        )

    def z1(self, h):
        x = self.p.x
        c = self.cp(0, h, x, 0, self.up)
        c.start()
        for what, k, dev in ((4, self.kr, self.right), (5, self.kl, self.left)):
            @pl.when(k == 0)
            def _():
                self.cp(what, h, x, 0, dev).start()

    def z2(self, h):
        x = self.p.x
        self.cp(0, h, x, 0, self.up).wait_recv()
        self.cp(1, h, x, 1, self.up).start()
        self.cp(2, h, x, 1, self.right).start()
        self.cp(3, h, x, 1, self.left).start()

    def z3(self, h):
        x = self.p.x
        self.cp(1, h, x, 1, self.up).wait_recv()
        for what, k, dev in ((4, self.kr, self.right), (5, self.kl, self.left)):
            @pl.when(k == 2)
            def _():
                self.cp(what, h, x, 2, dev).start()

    def far(self, h):
        self.cp(2, h, self.xl, 1, self.right).wait_recv()
        self.cp(3, h, self.xr, 1, self.left).wait_recv()
        self.cp(4, h, self.xl, kind(self.xl, self.p.x), self.right).wait_recv()
        self.cp(5, h, self.xr, kind(self.xr, self.p.x), self.left).wait_recv()
        self.cp(6, h, self.xl, self.fr, self.right).start()
        self.cp(7, h, self.xr, self.fl, self.left).start()

    def end(self, h):
        xf = (self.p.x + 2) % 4
        one = kind(xf, self.p.x)
        self.cp(6, h, xf, jnp.where(xf < 2, one, 1), self.right).wait_recv()
        self.cp(7, h, xf, jnp.where(xf < 2, 1, one), self.left).wait_recv()

    def sends(self, h):
        x = self.p.x
        for what in range(8):
            self.cp(what, h, x, 0, self.right).wait_send()


def rope(field, cosine, sine, sign):
    out = []
    for head in range(KVH):
        part = field[:, head * HD : (head + 1) * HD]
        out.append(part * cosine + sign * (pltpu.roll(part, HD // 2, 1) * sine))
    return jnp.concatenate(out, axis=1)


def forward_kernel(hid, w, v, cosine, sine, kb_o, vb_o, ha_o, ha, rel, wb, kb, vb, pcs, pcr, po, pys, pyr, send, recv, loc):
    p = Place()
    lo, y, c, zh, x, j = p.lo, p.y, p.c, p.zh, p.x, p.j
    copies = Copies(send, recv)
    yr, yl, yf = (y + 1) % 4, (y + 3) % 4, (y + 2) % 4
    mate = p.at(c=1 - c)
    xs = [(x + d) % 4 for d in (1, 3, 2)]
    peers = [mate]
    for yy in (yr, yl, yf):
        peers += [p.at(y=yy, c=0), p.at(y=yy, c=1)]
    peers += [p.at(x=xx) for xx in xs]
    peers += [p.z_next(), p.z_prev(), p.at(zh=(zh + 1) % 4), p.at(zh=(zh + 3) % 4)]

    part = x // 2 == c
    b = x % 2
    r = (zh - y + 4) % 4
    root = r == 0
    upward = ((r == 0) & (lo == 1)) | (r == 1) | ((r == 2) & (lo == 0))
    last = r == 2
    forward = part & jnp.logical_not(last)
    takes = part & jnp.logical_not(root)

    local_w = pltpu.make_async_copy(w, wb.at[b], loc.at[0])
    local_v = pltpu.make_async_copy(v, vb.at[x, 0], loc.at[1])
    local_h = pltpu.make_async_copy(hid.at[:, pl.ds(pl.multiple_of(j * 768, 128), 768)], ha.at[j], loc.at[2])

    @pl.when(part & root)
    def _():
        local_w.start()

    local_v.start()
    local_h.start()
    greet(peers)

    def piece(yy, cc):
        return hid.at[:, pl.ds(pl.multiple_of((2 * yy + cc) * 768, 128), 768)]

    i_rel = copies.new(2)
    rel_r = copies.make(piece(yf, 0), rel.at[0], i_rel, p.at(y=yr))
    rel_l = copies.make(piece(yf, 1), rel.at[1], i_rel + 1, p.at(y=yl))
    rel_r.start()
    rel_l.start()
    i_dir = copies.new(5)
    direct = []
    for n, (yy, cc) in enumerate(((yr, c), (yl, c), (yr, 1 - c), (yl, 1 - c), (y, 1 - c))):
        direct.append(copies.make(piece(yy, cc), ha.at[j], i_dir + n, p.at(y=yy, c=cc)))
    i_fw = copies.new(4)

    i_wz = copies.new(NQ)
    i_wx = copies.new(3 * NQ)
    rows = 384 // NQ

    def wz(q, dev):
        ref = wb.at[b, pl.ds(q * rows, rows), :]
        return copies.make(ref, ref, i_wz + q, dev)

    def wz_start(q):
        @pl.when(forward & upward)
        def _():
            wz(q, p.z_next()).start()

        @pl.when(forward & jnp.logical_not(upward))
        def _():
            wz(q, p.z_prev()).start()

    def wx(q, n, slot, dev):
        ref = wb.at[slot, pl.ds(q * rows, rows), :]
        return copies.make(ref, ref, i_wx + 3 * q + n, dev)

    def wx_start(q):
        @pl.when(part)
        def _():
            for n in (2, 0, 1):
                wx(q, n, b, p.at(x=xs[n])).start()

    @pl.when(part & root)
    def _():
        local_w.wait()

    for q in range(NQ):
        @pl.when(part & root)
        def _():
            wz_start(q)

    for d in direct:
        d.start()
    local_v.wait()
    gv = Gather(p, copies, vb)
    gv.z1(0)
    gv.z1(1)

    def w_step(q):
        @pl.when(takes)
        def _():
            wz(q, p.z_next()).wait_recv()
            wz_start(q)

        wx_start(q)

    w_step(0)
    w_step(1)
    rel_r.wait_recv()
    fw_r = copies.make(rel.at[0], ha.at[2 * yl + c], i_fw + c, p.at(y=yr, c=0))
    fw_r.start()
    rel_l.wait_recv()
    fw_l = copies.make(rel.at[1], ha.at[2 * yr + c], i_fw + 2 + c, p.at(y=yl, c=1))
    fw_l.start()
    w_step(2)
    w_step(3)
    gv.z2(0)
    gv.z2(1)

    for q in range(NQ):
        for slot in range(2):
            src = 2 * c + slot
            away = (src - x + 4) % 4
            for n, dist in ((0, 3), (1, 1), (2, 2)):
                @pl.when(away == dist)
                def _():
                    wx(q, n, slot, p.at(x=xs[n])).wait_recv()

    local_h.wait()
    for d in direct:
        d.wait_recv()
    for n in range(2):
        copies.make(rel.at[n], ha.at[2 * yf + n], i_fw + 2 * c + n, p.at(y=yr)).wait_recv()

    weights = wb[...].reshape(768, 512)

    i_pc = copies.new(4)
    order = (yf, yr, yl, y)
    to_mate = []
    for n, yy in enumerate(order):
        pcs[n] = jnp.dot(ha[2 * yy + 1 - c], weights, preferred_element_type=F32).astype(BF)
        cp = copies.make(pcs.at[n], pcr.at[n], i_pc + n, mate)
        cp.start()
        to_mate.append(cp)
    i_py = copies.new(3)
    to_y = []
    for n, yy in enumerate(order):
        own = jnp.dot(ha[2 * yy + c], weights, preferred_element_type=F32)
        to_mate[n].wait_recv()
        total = own + pcr[n].astype(F32)
        if n < 3:
            pys[n] = total.astype(BF)
            cp = copies.make(pys.at[n], pyr.at[n], i_py + n, p.at(y=yy))
            cp.start()
            to_y.append(cp)
        else:
            po[...] = total
    for cp in to_y:
        cp.wait_recv()
    raw = po[...] + pyr[0].astype(F32) + pyr[1].astype(F32) + pyr[2].astype(F32)
    kb[x, 0] = rope(raw, cosine[...], sine[...], 1.0).astype(BF)

    gk = Gather(p, copies, kb)
    both = (0, 1)
    for h in both:
        gk.z1(h)
    for h in both:
        gv.z3(h)
    for h in both:
        gk.z2(h)
    for h in both:
        gv.far(h)
    for h in both:
        gk.z3(h)
    for h in both:
        gk.far(h)
    for h in both:
        gv.end(h)
    ha_out = pltpu.make_async_copy(ha, ha_o, loc.at[3])
    vb_out = pltpu.make_async_copy(vb, vb_o, loc.at[4])
    ha_out.start()
    vb_out.start()
    for h in both:
        gk.end(h)
    kb_out = pltpu.make_async_copy(kb, kb_o, loc.at[5])
    kb_out.start()

    rel_r.wait_send()
    rel_l.wait_send()
    for cp in direct + [fw_r, fw_l] + to_mate + to_y:
        cp.wait_send()
    for q in range(NQ):
        @pl.when(forward)
        def _():
            wz(q, p.z_next()).wait_send()

        @pl.when(part)
        def _():
            for n in range(3):
                wx(q, n, b, p.at(x=xs[n])).wait_send()
    for h in both:
        gv.sends(h)
        gk.sends(h)
    ha_out.wait()
    vb_out.wait()
    kb_out.wait()


def attention_kernel(q, do, k, v, qd, kd, out, dq, dk, dv, probs, ds_all, bias, kc, vc, qs, dos):
    x = lax.axis_index("seq") % 4
    rows = q.shape[0]
    keys = kd.shape[1]
    scale = 1.0 / math.sqrt(HD)

    @pl.when(pl.program_id(0) == 0)
    def _():
        row = lax.broadcasted_iota(jnp.int32, (rows, keys), 0)
        col = lax.broadcasted_iota(jnp.int32, (rows, keys), 1)
        seen = (qd[...] == kd[...]) & (col - (keys - rows) <= row)
        bias[...] = jnp.where(seen, 0.0, -1e30)

    for n in range(9):
        xs, kk = (x + n) % 4, 2 - (x + n) // 4
        kc[n * rows : (n + 1) * rows] = k[xs, kk]
        vc[n * rows : (n + 1) * rows] = v[xs, kk]
    nt = (((1,), (1,)), ((), ()))
    tn = (((0,), (0,)), ((), ()))
    for h in range(GROUP):
        at = slice(h * HD, (h + 1) * HD)
        to = slice(h * rows, (h + 1) * rows)
        qh = q[:, at]
        doh = do[:, at]
        qs[to] = qh
        dos[to] = doh
        s = lax.dot_general(qh, kc[...], nt, preferred_element_type=F32)
        w = jnp.exp2(s * (scale * math.log2(math.e)) + bias[...])
        total = jnp.sum(w, axis=1, keepdims=True)
        inverse = 1.0 / total
        mixed = jnp.dot(w.astype(BF), vc[...], preferred_element_type=F32)
        attended = (mixed * inverse).astype(BF)
        out[:, at] = attended
        delta = jnp.sum(doh.astype(F32) * attended.astype(F32), axis=1, keepdims=True)
        prob = w * inverse
        probs[to] = prob.astype(BF)
        dprob = lax.dot_general(doh, vc[...], nt, preferred_element_type=F32)
        ds = (prob * (dprob - delta)).astype(BF)
        ds_all[to] = ds
        dq[:, at] = (jnp.dot(ds, kc[...], preferred_element_type=F32) * scale).astype(BF)
    dvc = lax.dot_general(probs[...], dos[...], tn, preferred_element_type=F32).astype(BF)
    dkc = (lax.dot_general(ds_all[...], qs[...], tn, preferred_element_type=F32) * scale).astype(BF)
    for n in range(9):
        xs, kk = (x + n) % 4, 2 - (x + n) // 4
        dk[xs, kk] = dkc[n * rows : (n + 1) * rows]
        dv[xs, kk] = dvc[n * rows : (n + 1) * rows]


class Scatter:
    def __init__(self, place, copies, buf, rn, rz, zs, acc):
        self.p, self.copies, self.buf = place, copies, buf
        self.rn, self.rz, self.zs, self.acc = rn, rz, zs, acc
        p = place
        x = p.x
        self.xl, self.xr, self.xf = (x + 3) % 4, (x + 1) % 4, (x + 2) % 4
        self.left, self.right = p.at(x=self.xl), p.at(x=self.xr)
        self.down = p.at(zh=(p.zh + 3) % 4)
        self.base = copies.new(16)

    def cp(self, what, h, src, dst, device):
        at = pl.ds(256 * h, 256)
        return self.copies.make(src.at[:, at], dst.at[:, at], self.base + 2 * what + h, device)

    def start(self, h):
        x, xl, xr, xf = self.p.x, self.xl, self.xr, self.xf
        buf, rn = self.buf, self.rn
        one = kind(xf, x)
        self.cp(0, h, buf.at[xf, jnp.where(xf < 2, one, 1)], rn.at[0], self.left).start()
        self.cp(1, h, buf.at[xf, jnp.where(xf < 2, 1, one)], rn.at[1], self.right).start()
        self.cp(2, h, buf.at[xl, jnp.where(xl < 2, 1, kind(xl, x))], rn.at[2], self.left).start()
        self.cp(3, h, buf.at[xr, jnp.where(xr < 2, kind(xr, x), 1)], rn.at[3], self.right).start()

    def add(self, h):
        x, xl, xr = self.p.x, self.xl, self.xr
        buf, rn = self.buf, self.rn
        at = pl.ds(256 * h, 256)
        for what, target, k, dev in (
            (0, xl, jnp.where(xl < 2, kind(xl, x), 1), self.left),
            (1, xr, jnp.where(xr < 2, 1, kind(xr, x)), self.right),
        ):
            self.cp(what, h, rn.at[what], rn.at[what], dev).wait_recv()
            both = buf[target, k, :, at].astype(F32) + rn[what, :, at].astype(F32)
            self.zs[what, :, at] = both.astype(BF)
            self.cp(4 + what, h, self.zs.at[what], rn.at[4 + what], dev).start()

    def own(self, h):
        x, xl, xr = self.p.x, self.xl, self.xr
        at = pl.ds(256 * h, 256)
        for k in range(3):
            self.acc[k, :, at] = self.buf[x, k, :, at].astype(F32)
        for what, k in (
            (2, jnp.where(x < 2, 1, kind(x, xr))),
            (3, jnp.where(x < 2, kind(x, xl), 1)),
            (4, jnp.where(x < 2, kind(x, xr), 1)),
            (5, jnp.where(x < 2, 1, kind(x, xl))),
        ):
            self.cp(what, h, self.rn.at[what], self.rn.at[what], self.left).wait_recv()
            self.acc[k, :, at] += self.rn[what, :, at].astype(F32)
        self.zs[2, :, at] = self.acc[2, :, at].astype(BF)
        self.cp(6, h, self.zs.at[2], self.rz.at[0], self.down).start()

    def z2(self, h):
        at = pl.ds(256 * h, 256)
        self.cp(6, h, self.rz.at[0], self.rz.at[0], self.down).wait_recv()
        self.zs[3, :, at] = (self.acc[1, :, at] + self.rz[0, :, at].astype(F32)).astype(BF)
        self.cp(7, h, self.zs.at[3], self.rz.at[1], self.down).start()

    def end(self, h):
        at = pl.ds(256 * h, 256)
        self.cp(7, h, self.rz.at[1], self.rz.at[1], self.down).wait_recv()
        self.acc[0, :, at] += self.rz[1, :, at].astype(F32)

    def sends(self, h):
        for what in range(8):
            self.cp(what, h, self.rn.at[0], self.rn.at[0], self.left).wait_send()


def backward_kernel(
    dkb, dvb, ha, cosine, sine, gv_o, gw_o,
    krn, krz, kzs, kacc, vrn, vrz, vzs, vacc, kga, wg, wx1, wx2, wzr, wsum, wfin, send, recv,
):
    p = Place()
    lo, y, c, zh, x, j = p.lo, p.y, p.c, p.zh, p.x, p.j
    copies = Copies(send, recv)
    yr, yl, yf = (y + 1) % 4, (y + 3) % 4, (y + 2) % 4
    xl, xr = (x + 3) % 4, (x + 1) % 4
    mate = p.at(c=1 - c)
    up_z, down_z = p.z_next(), p.z_prev()
    greet(
        [mate, p.at(y=yr), p.at(y=yl), p.at(y=yf), p.at(x=xl), p.at(x=xr), up_z, down_z]
        + [p.at(zh=(zh + 1) % 4), p.at(zh=(zh + 3) % 4)]
    )
    sk = Scatter(p, copies, dkb, krn, krz, kzs, kacc)
    sv = Scatter(p, copies, dvb, vrn, vrz, vzs, vacc)
    both = (0, 1)
    for h in both:
        sk.start(h)
    for h in both:
        sk.add(h)
    for h in both:
        sk.own(h)
    for h in both:
        sv.start(h)
    for h in both:
        sk.z2(h)
    for h in both:
        sv.add(h)
    for h in both:
        sk.end(h)

    kga[j] = rope(kacc[0], cosine[...], sine[...], -1.0).astype(BF)
    i_ky = copies.new(4)
    i_kc = copies.new(3)
    gives = []
    for n, yy in enumerate((yf, yr, yl)):
        gives.append(copies.make(kga.at[j], kga.at[j], i_ky + n, p.at(y=yy)))
    gives.append(copies.make(kga.at[j], kga.at[j], i_ky + 3, mate))
    for cp in gives:
        cp.start()
    passes = []
    for n, yy in ((1, yl), (2, yr), (0, yf)):
        gives[n].wait_recv()
        ref = kga.at[2 * yy + c]
        cp = copies.make(ref, ref, i_kc + n, mate)
        cp.start()
        passes.append(cp)
    gives[3].wait_recv()
    for h in both:
        sv.own(h)
    for cp in passes:
        cp.wait_recv()

    tn = (((0,), (0,)), ((), ()))
    tokens = kga[...].reshape(1024, 512)
    rows = 384 // NQ
    u = (x - 2 * c + 4) % 4
    given = jnp.where((u == 0) | (u == 3), 1, 0)
    kept = 1 - given
    even = u % 2 == 0
    ends = u < 2
    r = (zh - y + 4) % 4
    root = r == 0
    upward = ((r == 0) & (lo == 1)) | (r == 1) | ((r == 2) & (lo == 0))
    i_x1 = copies.new(NQ)
    i_x2 = copies.new(NQ)
    i_z = copies.new(NQ)
    i_l = copies.new(NQ)
    i_y = copies.new(3 * NQ)
    i_c = copies.new(NQ)
    sl = [pl.ds(q * rows, rows) for q in range(NQ)]

    def x1(q, dev):
        return copies.make(wg.at[given, sl[q], :], wx1.at[sl[q], :], i_x1 + q, dev)

    def x2(q, dev):
        return copies.make(wsum.at[sl[q], :], wx2.at[sl[q], :], i_x2 + q, dev)

    def zc(q, dev):
        return copies.make(wsum.at[sl[q], :], wzr.at[0, sl[q], :], i_z + q, dev)

    def lc(q):
        return copies.make(wsum.at[sl[q], :], wzr.at[1, sl[q], :], i_l + q, p.at(lo=1 - lo))

    def yc(q, n, yy):
        return copies.make(wfin.at[sl[q], :], wfin.at[sl[q], :], i_y + 3 * q + n, p.at(y=yy))

    def cc(q):
        return copies.make(wfin.at[sl[q], :], wfin.at[sl[q], :], i_c + q, mate)

    wide = ha[...].reshape(1024, 768)
    wg[...] = lax.dot_general(wide, tokens, tn, preferred_element_type=F32).reshape(2, 384, 512).astype(BF)
    for q in range(NQ):
        @pl.when(even)
        def _():
            x1(q, p.at(x=xr)).start()

        @pl.when(jnp.logical_not(even))
        def _():
            x1(q, p.at(x=xl)).start()

    for q in range(NQ):
        x1(q, p.at(x=xr)).wait_recv()
        wsum[sl[q], :] = (wg[kept, sl[q], :].astype(F32) + wx1[sl[q], :].astype(F32)).astype(BF)

        @pl.when(u == 2)
        def _():
            x2(q, p.at(x=xl)).start()

        @pl.when(u == 3)
        def _():
            x2(q, p.at(x=xr)).start()

    for h in both:
        sv.z2(h)

    for q in range(NQ):
        @pl.when(ends)
        def _():
            x2(q, p.at(x=xr)).wait_recv()
            total = wsum[sl[q], :].astype(F32) + wx2[sl[q], :].astype(F32)

            @pl.when(r == 2)
            def _():
                wsum[sl[q], :] = total.astype(BF)

            @pl.when(r != 2)
            def _():
                zc(q, up_z).wait_recv()
                wsum[sl[q], :] = (total + wzr[0, sl[q], :].astype(F32)).astype(BF)

            @pl.when(jnp.logical_not(root) & upward)
            def _():
                zc(q, down_z).start()

            @pl.when(jnp.logical_not(root) & jnp.logical_not(upward))
            def _():
                zc(q, up_z).start()

            @pl.when(root)
            def _():
                lc(q).start()

    for q in range(NQ):
        @pl.when(ends & root)
        def _():
            lc(q).wait_recv()
            total = wsum[sl[q], :].astype(F32) + wzr[1, sl[q], :].astype(F32)
            wfin[sl[q], :] = (total * (1.0 / 16.0)).astype(BF)
            for n, yy in enumerate((yf, yr, yl)):
                yc(q, n, yy).start()
            cc(q).start()

    away = (zh - y + 4) % 4
    for q in range(NQ):
        @pl.when(ends & jnp.logical_not(root))
        def _():
            for n, dist in ((0, 2), (1, 3), (2, 1)):
                @pl.when(away == dist)
                def _():
                    yc(q, n, yf).wait_recv()
            cc(q).start()

        @pl.when(jnp.logical_not(ends))
        def _():
            cc(q).wait_recv()

        gw_o[sl[q], :] = wfin[sl[q], :].astype(F32)

    for h in both:
        sv.end(h)
    gv_o[...] = vacc[0].astype(BF)

    for cp in gives + passes:
        cp.wait_send()
    for q in range(NQ):
        x1(q, p.at(x=xr)).wait_send()

        @pl.when(jnp.logical_not(ends))
        def _():
            x2(q, p.at(x=xr)).wait_send()

        @pl.when(ends)
        def _():
            cc(q).wait_send()

            @pl.when(root)
            def _():
                lc(q).wait_send()
                for n, yy in enumerate((yf, yr, yl)):
                    yc(q, n, yy).wait_send()

            @pl.when(jnp.logical_not(root))
            def _():
                zc(q, up_z).wait_send()
    for h in both:
        sk.sends(h)
        sv.sends(h)


def vmem():
    return pl.BlockSpec(memory_space=pltpu.VMEM)


def local(inputs, queries, values, key_weight, doc_ids, grad_out):
    rows = inputs.shape[1]
    width = 512
    sq = lax.axis_index("seq")
    positions = sq * rows + jnp.arange(rows)
    half = HD // 2
    freqs = ROPE_BASE ** (-(jnp.arange(half).astype(F32) * 2.0 / HD))
    angles = positions.astype(F32)[:, None] * freqs[None, :]
    cos, sin = jnp.cos(angles), jnp.sin(angles)
    cosine = jnp.concatenate([cos, cos], axis=1)
    sine = jnp.concatenate([-sin, sin], axis=1)

    any_spec = pl.BlockSpec(memory_space=pl.ANY)
    dma = pltpu.SemaphoreType.DMA
    blocks = (4, 3, rows, width)
    kb, vb, ha = pl.pallas_call(
        forward_kernel,
        out_shape=(
            jax.ShapeDtypeStruct(blocks, BF),
            jax.ShapeDtypeStruct(blocks, BF),
            jax.ShapeDtypeStruct((8, rows, 768), BF),
        ),
        in_specs=[any_spec, any_spec, any_spec, vmem(), vmem()],
        out_specs=(any_spec, any_spec, any_spec),
        scratch_shapes=[
            pltpu.VMEM((8, rows, 768), BF),
            pltpu.VMEM((2, rows, 768), BF),
            pltpu.VMEM((2, 384, width), BF),
            pltpu.VMEM(blocks, BF),
            pltpu.VMEM(blocks, BF),
            pltpu.VMEM((4, rows, width), BF),
            pltpu.VMEM((4, rows, width), BF),
            pltpu.VMEM((rows, width), F32),
            pltpu.VMEM((3, rows, width), BF),
            pltpu.VMEM((3, rows, width), BF),
            dma((96,)),
            dma((96,)),
            dma((6,)),
        ],
        compiler_params=pltpu.CompilerParams(
            collective_id=0, has_side_effects=True, vmem_limit_bytes=VMEM_LIMIT
        ),
        name="forward_exchange",
    )(inputs[0], key_weight, values[0], cosine, sine)

    keys = 9 * rows
    padded = jnp.concatenate([jnp.full((8 * rows,), -1, jnp.int32), doc_ids[0]])
    key_docs = lax.dynamic_slice_in_dim(padded, sq * rows, keys, 0)
    query_docs = key_docs[8 * rows :]
    head = GROUP * HD
    attn, dq, dkb, dvb = pl.pallas_call(
        attention_kernel,
        grid=(KVH,),
        out_shape=(
            jax.ShapeDtypeStruct((rows, QH * HD), BF),
            jax.ShapeDtypeStruct((rows, QH * HD), BF),
            jax.ShapeDtypeStruct(blocks, BF),
            jax.ShapeDtypeStruct(blocks, BF),
        ),
        in_specs=[
            pl.BlockSpec((rows, head), lambda g: (0, g)),
            pl.BlockSpec((rows, head), lambda g: (0, g)),
            pl.BlockSpec((4, 3, rows, HD), lambda g: (0, 0, 0, g)),
            pl.BlockSpec((4, 3, rows, HD), lambda g: (0, 0, 0, g)),
            pl.BlockSpec((rows, 1), lambda g: (0, 0)),
            pl.BlockSpec((1, keys), lambda g: (0, 0)),
        ],
        out_specs=(
            pl.BlockSpec((rows, head), lambda g: (0, g)),
            pl.BlockSpec((rows, head), lambda g: (0, g)),
            pl.BlockSpec((4, 3, rows, HD), lambda g: (0, 0, 0, g)),
            pl.BlockSpec((4, 3, rows, HD), lambda g: (0, 0, 0, g)),
        ),
        scratch_shapes=[
            pltpu.VMEM((GROUP * rows, keys), BF),
            pltpu.VMEM((GROUP * rows, keys), BF),
            pltpu.VMEM((rows, keys), F32),
            pltpu.VMEM((keys, HD), BF),
            pltpu.VMEM((keys, HD), BF),
            pltpu.VMEM((GROUP * rows, HD), BF),
            pltpu.VMEM((GROUP * rows, HD), BF),
        ],
        compiler_params=pltpu.CompilerParams(vmem_limit_bytes=VMEM_LIMIT),
        name="attention",
    )(queries[0], grad_out[0], kb, vb, query_docs[:, None], key_docs[None, :])

    block = (rows, width)
    per_sum = [
        pltpu.VMEM((6,) + block, BF),
        pltpu.VMEM((2,) + block, BF),
        pltpu.VMEM((4,) + block, BF),
        pltpu.VMEM((3,) + block, F32),
    ]
    grad_values, weight_grad = pl.pallas_call(
        backward_kernel,
        out_shape=(
            jax.ShapeDtypeStruct(block, BF),
            jax.ShapeDtypeStruct((384, width), F32),
        ),
        in_specs=[vmem()] * 5,
        out_specs=(vmem(), vmem()),
        scratch_shapes=per_sum
        + per_sum
        + [
            pltpu.VMEM((8,) + block, BF),
            pltpu.VMEM((2, 384, width), BF),
            pltpu.VMEM((384, width), BF),
            pltpu.VMEM((384, width), BF),
            pltpu.VMEM((2, 384, width), BF),
            pltpu.VMEM((384, width), BF),
            pltpu.VMEM((384, width), BF),
            dma((80,)),
            dma((80,)),
        ],
        compiler_params=pltpu.CompilerParams(
            collective_id=1, has_side_effects=True, vmem_limit_bytes=VMEM_LIMIT
        ),
        name="backward_exchange",
    )(dkb, dvb, ha, cosine, sine)
    return attn[None], dq[None], grad_values[None], weight_grad


def solution(mesh):
    in_specs = (
        P("dp", "seq", None),
        P("dp", "seq", None),
        P("dp", "seq", None),
        P("seq", None),
        P("dp", None),
        P("dp", "seq", None),
    )
    out_specs = (P("dp", "seq", None), P("dp", "seq", None), P("dp", "seq", None), P("seq", None))
    return jax.shard_map(local, mesh=mesh, in_specs=in_specs, out_specs=out_specs, check_vma=False)
```

time: 785 us -> 178 us (0.23)
  waiting for transfers between devices: 588 us -> 0 us
  Pallas kernels: 0 us -> 170 us
  local copies, waits for them, and re-layouts: 94.3 us -> 6.5 us
  matrix products: 61.3 us -> 0 us
  other arithmetic: 19.4 us -> 1.08 us
  between operations: 14.3 us -> 0.67 us
    reduce_scatter x2 -> x0, waiting for transfers between devices: 278 us -> none  [the longest x1 159 us: local(): lax.psum_scatter(lax.dot_general(hidden, key_grad_raw, (((0,), (0,)), (()...]
    all_gather x3 -> x0, waiting for transfers between devices: 195 us -> none  [the longest x1 101 us: local(): lax.all_gather(key_weight, 'seq', axis=0, tiled=True)]
    pallas_call x0 -> x3, Pallas kernels: none -> 170 us  [the longest x1 83.9 us: local(): pl.pallas_call(backward_kernel, out_shape=(jax.ShapeDtypeStruct(block, BF...]
    psum x1 -> x0, waiting for transfers between devices: 114 us -> none  [local(): weight_grad = lax.psum(partial_grad, 'dp') / lax.axis_size('dp')]
    dot_general x30 -> x0, matrix products: 61.3 us -> none  [the longest x8 22.3 us: exp_weights(): jnp.einsum('tkgd,ckd->kgtc', query_heads, key_tile, preferred_element_typ...]
    dynamic_slice x29 -> x1, local copies, waits for them, and re-layouts: 26.4 us -> 0.78 us  [local(): key_docs = lax.dynamic_slice_in_dim(padded, sq * rows, keys, 0)]
    dynamic_update_slice x8 -> x0, local copies, waits for them, and re-layouts: 24.4 us -> none  [local(): lax.scan(backward_step, zero_mix, (key_tiles, value_tiles, doc_tiles, anc...]
    unnamed x18 -> x2, local copies, waits for them, and re-layouts: 16.5 us -> 3.63 us
  transfers between devices with their start and end apart: 6 -> 0, of which waited for: 6 -> 0; matrix products, arithmetic and copies ran while one was open for 4% -> 0% of each run, Pallas kernels for 0% -> 0%
where the time goes in v1:
time: 178 us
  Pallas kernels  170 us (96%)
  local copies, waits for them, and re-layouts  6.5 us (4%)
    pallas_call x1, Pallas kernels, local(): pl.pallas_call(backward_kernel, out_shape=(jax.ShapeDtypeStruct(block, BF...  83.9 us
    pallas_call x1, Pallas kernels, local(): pl.pallas_call(forward_kernel, out_shape=(jax.ShapeDtypeStruct(blocks, BF...  66.1 us
    pallas_call x1, Pallas kernels, local(): pl.pallas_call(attention_kernel, grid=(KVH,), out_shape=(jax.ShapeDtypeSt...  19.6 us
    unnamed x2, local copies, waits for them, and re-layouts  3.63 us

profile of v1, /device:TPU:9, one launch (start us, length us, event | category | flops | bytes accessed | tf_op | source)
XLA Modules:
  0.0 177.9 jit_solution(10131956176733496630)
XLA Ops:
  0.6 0.8 fusion.1
  1.4 0.8 pad_dynamic-slice_fusion.1
  2.2 0.6 broadcast_in_dim.19.kd
  2.8 0.7 copy.10.qd
  3.5 0.3 fusion
  3.8 0.8 pad_maximum_fusion
  4.6 66.1 %forward_exchange.1 = (bf16[4,3,128,512]{3,2,1,0:T(8,128)(2,1)}, bf16[4,3,128,512]{3,2,1,0:T(8,128)(2,1)}, bf16[8,128,768]{2,1,0:T(8,128)(2,1)}) custom-call(bf16[128,6144]{1,0:T(8,128)(2,1)} %bitcast.10, bf16[384,512]{1,0:T(8,128)(2,1)} %w.1, bf16[128,512]{1,0:T(8,128)(2,1)} %bitcast.13, f32[128,128]{1,0:T(8,128)} %get-tuple-element.25.cosine, ...), custom_call_target="tpu_custom_call" | custom-call | tf_op jit(solution)/shard_map/forward_exchange/pallas_call | solution.py:691
  70.7 19.6 %attention.1 = (bf16[128,3072]{1,0:T(8,128)(2,1)}, bf16[128,3072]{1,0:T(8,128)(2,1)}, bf16[4,3,128,512]{3,2,1,0:T(8,128)(2,1)}, bf16[4,3,128,512]{3,2,1,0:T(8,128)(2,1)}) custom-call(bf16[128,3072]{1,0:T(8,128)(2,1)} %bitcast.11, bf16[128,3072]{1,0:T(8,128)(2,1)} %bitcast.12, bf16[4,3,128,512]{3,2,1,0:T(8,128)(2,1)} %get-tuple-element.13.k, ...), custom_call_target="tpu_custom_call" | custom-call | tf_op jit(solution)/shard_map/attention/pallas_call | solution.py:726
  90.3 83.9 %backward_exchange.1 = (bf16[128,512]{1,0:T(8,128)(2,1)}, f32[384,512]{1,0:T(8,128)}) custom-call(bf16[4,3,128,512]{3,2,1,0:T(8,128)(2,1)} %get-tuple-element.17.dkb, bf16[4,3,128,512]{3,2,1,0:T(8,128)(2,1)} %get-tuple-element.18.dvb, bf16[8,128,768]{2,1,0:T(8,128)(2,1)} %get-tuple-element.19.ha, f32[128,128]{1,0:T(8,128)} %get-tuple-element.25.cosine, ...), custom_call_target="tpu_custom_call" | custom-call | tf_op jit(solution)/shard_map/backward_exchange/pallas_call | solution.py:769
  174.3 1.6 copy.13
  175.9 2.1 %copy.14 = f32[384,512]{1,0:T(8,128)} copy(f32[384,512]{1,0:T(8,128)} %get-tuple-element.34) | data formatting | bytes 1572864
  (2 shorter events, 0.0 us)

commit v2 on v0

v2 whole, which is shorter than its diff:
```python
import math

import jax
import jax.numpy as jnp
import numpy as np
from jax import lax
from jax.experimental import pallas as pl
from jax.experimental.pallas import tpu as pltpu
from jax.sharding import PartitionSpec as P

QH = 24
KVH = 4
HD = 128
GROUP = QH // KVH
ROPE_BASE = 1000000.0
MESH = pl.DeviceIdType.MESH
BF = jnp.bfloat16
F32 = jnp.float32
NQ = 4
SENDS = 21
RECVS = 78
VMEM_LIMIT = 56 * 1024 * 1024


class Place:
    def __init__(self):
        dp = lax.axis_index("dp")
        sq = lax.axis_index("seq")
        self.lo = dp // 8
        self.y = (dp // 2) % 4
        self.c = dp % 2
        self.zh = sq // 4
        self.x = sq % 4
        self.j = dp % 8

    def at(self, lo=None, y=None, c=None, zh=None, x=None):
        lo = self.lo if lo is None else lo
        y = self.y if y is None else y
        c = self.c if c is None else c
        zh = self.zh if zh is None else zh
        x = self.x if x is None else x
        return (lo * 8 + y * 2 + c, zh * 4 + x)

    def z_next(self):
        return self.at(lo=1 - self.lo, zh=(self.zh + self.lo) % 4)

    def z_prev(self):
        return self.at(lo=1 - self.lo, zh=(self.zh + 3 + self.lo) % 4)


class Copies:
    def __init__(self, send, recv, other):
        self.send, self.recv, self.other = send, recv, other
        self.sends = self.recvs = 0

    def new_send(self, number=1):
        self.sends += number
        return self.sends - number

    def new_recv(self, number=1):
        self.recvs += number
        return self.recvs - number

    def make(self, src, dst, send, recv, device):
        return pltpu.make_async_remote_copy(
            src_ref=src,
            dst_ref=dst,
            send_sem=self.send.at[send],
            recv_sem=self.recv.at[recv],
            device_id=device,
            device_id_type=MESH,
        )

    def sent(self, ref, send):
        self.make(ref, ref, send, 0, self.other).wait_send()

    def got(self, ref, recv):
        self.make(ref, ref, 0, recv, self.other).wait_recv()


def greet(devices):
    barrier = pltpu.get_barrier_semaphore()
    for device in devices:
        pl.semaphore_signal(barrier, inc=1, device_id=device, device_id_type=MESH)
    pl.semaphore_wait(barrier, len(devices))


def kind(source, reader):
    return jnp.where(reader > source, 0, 2)


class Gather:
    def __init__(self, place, copies, buf):
        self.p, self.copies, self.buf = place, copies, buf
        self.out = copies.new_send()
        self.base = copies.new_recv(3 * KVH)

    def cp(self, what, g, k, to, device):
        x = self.p.x
        index = self.base + KVH * what + g
        self.copies.make(self.buf.at[g, x, k], self.buf.at[g, x, to], self.out, index, device).start()

    def across(self, g, k):
        p = self.p
        for d in (2, 1, 3):
            to = (p.x + d) % 4
            if k == 1:
                self.cp(2, g, 1, 1, p.at(x=to))
            else:
                @pl.when(kind(p.x, to) == k)
                def _():
                    self.cp(2, g, k, k, p.at(x=to))

    def start(self, g):
        p = self.p
        self.cp(0, g, 0, 1, p.at(zh=(p.zh + 1) % 4))
        self.cp(1, g, 0, 2, p.at(zh=(p.zh + 2) % 4))
        self.across(g, 0)

    def pass_on(self, g):
        for what in (0, 1):
            self.copies.got(self.buf.at[g, self.p.x, what + 1], self.base + KVH * what + g)
            self.across(g, what + 1)

    def end(self, g):
        self.copies.got(self.buf.at[g, 0:2], self.base + 2 * KVH + g)

    def sends(self):
        self.copies.sent(self.buf.at[:, :, 0:2], self.out)


class Scatter:
    def __init__(self, place, copies, buf, rn, rz, zs, acc):
        self.p, self.copies, self.buf = place, copies, buf
        self.rn, self.rz, self.zs, self.acc = rn, rz, zs, acc
        self.out = copies.new_send(2)
        self.base = copies.new_recv(2 * KVH)

    def start(self, g):
        p = self.p
        for d in (2, 1, 3):
            to = (p.x + d) % 4
            for slot, k in ((d - 1, kind(to, p.x)), (2 + d, 1)):
                self.copies.make(
                    self.buf.at[g, to, k], self.rn.at[g, slot], self.out, self.base + g, p.at(x=to)
                ).start()

    def across(self, g):
        p = self.p
        acc = self.acc
        self.copies.got(self.rn.at[g], self.base + g)
        for k in range(3):
            acc[g, k] = self.buf[g, p.x, k].astype(F32)
        for d in (1, 3, 2):
            k = kind(p.x, (p.x + 4 - d) % 4)
            acc[g, k] += self.rn[g, d - 1].astype(F32)
            acc[g, 1] += self.rn[g, 2 + d].astype(F32)
        for n, back in ((1, 2), (0, 3)):
            self.zs[g, n] = acc[g, n + 1].astype(BF)
            self.copies.make(
                self.zs.at[g, n], self.rz.at[g, n], self.out + 1, self.base + KVH + g, p.at(zh=(p.zh + back) % 4)
            ).start()

    def end(self, g):
        self.copies.got(self.rz.at[g], self.base + KVH + g)
        return self.acc[g, 0] + self.rz[g, 0].astype(F32) + self.rz[g, 1].astype(F32)

    def sends(self):
        self.copies.sent(self.rn, self.out)
        self.copies.sent(self.rz, self.out + 1)


def spread(table):
    lane = lax.broadcasted_iota(jnp.int32, table.shape, 1)
    turned = pltpu.roll(table, HD // 2, 1)
    return jnp.where(lane < HD // 2, table, turned), jnp.where(lane < HD // 2, -turned, table)


def rope(part, cosine, sine, sign):
    return part * cosine + sign * (pltpu.roll(part, HD // 2, 1) * sine)


def whole_kernel(
    hid, w, v, q_in, do_in, docs, table,
    out_o, dq_o, gv_o, gw_o,
    q, do, out, dq,
    ha, hat, wb, kb, vb, po, pcs, pcr, pys, pyr, tab,
    probs, ds_all, bias, kc, vc, qs, dos,
    dkb, dvb, krn, vrn, krz, vrz, kzs, vzs, kacc, vacc,
    kga, wg, wxr, wsum, wzr, wlo, wlr, wfin,
    send, recv, loc,
):
    p = Place()
    lo, y, c, zh, x, j = p.lo, p.y, p.c, p.zh, p.x, p.j
    yr, yl, yf = (y + 1) % 4, (y + 3) % 4, (y + 2) % 4
    mate = p.at(c=1 - c)
    copies = Copies(send, recv, mate)
    up_z, down_z = p.z_next(), p.z_prev()
    xs = [(x + d) % 4 for d in (1, 3, 2)]
    peers = [mate]
    for yy in (yr, yl, yf):
        peers += [p.at(y=yy, c=0), p.at(y=yy, c=1)]
    peers += [p.at(x=xx) for xx in xs]
    for d in (1, 2, 3):
        peers += [p.at(zh=(zh + d) % 4), p.at(zh=(zh + d) % 4, lo=1 - lo)]
    peers.append(p.at(lo=1 - lo))
    rows = HD
    scale = 1.0 / math.sqrt(HD)

    part = x // 2 == c
    b = x % 2
    r = (zh - y + 4) % 4
    root = r == 0
    upward = ((r == 0) & (lo == 1)) | (r == 1) | ((r == 2) & (lo == 0))
    forward = part & (r != 2)
    takes = part & jnp.logical_not(root)

    local_w = pltpu.make_async_copy(w, wb.at[b], loc.at[0])
    local_h = pltpu.make_async_copy(hid.at[:, pl.ds(pl.multiple_of(j * 768, 128), 768)], ha.at[y, c], loc.at[1])
    place = pl.multiple_of((zh * 4 + x) * rows, rows)
    local_t = pltpu.make_async_copy(table.at[pl.ds(place, rows), :], tab, loc.at[2])
    local_q = pltpu.make_async_copy(q_in, q, loc.at[3])
    local_do = pltpu.make_async_copy(do_in, do, loc.at[4])
    local_v = [
        pltpu.make_async_copy(v.at[:, g * HD : (g + 1) * HD], vb.at[g, x, 0], loc.at[5 + g]) for g in range(KVH)
    ]

    @pl.when(part & root)
    def _():
        local_w.start()

    local_h.start()
    for cp in local_v:
        cp.start()
    local_t.start()
    local_q.start()
    local_do.start()
    greet(peers)

    def piece(yy, cc):
        return hid.at[:, pl.ds(pl.multiple_of((2 * yy + cc) * 768, 128), 768)]

    s_wz, r_wz = copies.new_send(NQ), copies.new_recv(NQ)
    s_wx, r_wx = copies.new_send(), copies.new_recv()
    wrows = 384 // NQ

    def wpart(n):
        return wb.at[b, pl.ds(n * wrows, wrows), :]

    def w_start(n):
        ref = wpart(n)

        @pl.when(forward & upward)
        def _():
            copies.make(ref, ref, s_wz + n, r_wz + n, up_z).start()

        @pl.when(forward & jnp.logical_not(upward))
        def _():
            copies.make(ref, ref, s_wz + n, r_wz + n, down_z).start()

        @pl.when(part)
        def _():
            for m in (2, 0, 1):
                copies.make(ref, ref, s_wx, r_wx, p.at(x=xs[m])).start()

    @pl.when(part & root)
    def _():
        local_w.wait()
        w_start(0)
        w_start(1)

    seven = hat.at[0:672]
    s_dir, r_dir = copies.new_send(), copies.new_recv()
    for yy, cc in ((yf, c), (yf, 1 - c), (yr, c), (yr, 1 - c), (yl, c), (yl, 1 - c), (y, 1 - c)):
        copies.make(piece(yy, cc), ha.at[y, c], s_dir, r_dir, p.at(y=yy, c=cc)).start()

    @pl.when(part & root)
    def _():
        for n in range(2, NQ):
            copies.sent(wpart(n - 2), s_wz + n - 2)
            w_start(n)

    gv = Gather(p, copies, vb)
    gk = Gather(p, copies, kb)

    @pl.when(takes)
    def _():
        for n in range(NQ):
            copies.got(wpart(n), r_wz + n)
            w_start(n)

    for cp in local_v:
        cp.wait()
    gv.start(0)

    @pl.when(part)
    def _():
        copies.got(wb.at[0], r_wx)

    @pl.when(jnp.logical_not(part))
    def _():
        copies.got(wb, r_wx)

    gv.start(1)
    gv.start(2)
    gv.start(3)
    gv.pass_on(0)
    local_h.wait()
    local_t.wait()
    cosine, sine = spread(tab[...])
    s_pc, r_pc = copies.new_send(), copies.new_recv(2)
    s_py, r_py = copies.new_send(), copies.new_recv(2)
    copies.got(seven, r_dir)
    for half in range(2):
        weights = wb[:, :, half * 256 : (half + 1) * 256].reshape(768, 256)
        theirs = jnp.dot(ha[:, 1 - c].reshape(512, 768), weights, preferred_element_type=F32)
        pcs[half] = theirs.astype(BF).reshape(4, rows, 256)
        copies.make(pcs.at[half], pcr.at[half], s_pc, r_pc + half, mate).start()
        po[half] = jnp.dot(ha[:, c].reshape(512, 768), weights, preferred_element_type=F32).reshape(4, rows, 256)
    for half in range(2):
        copies.got(pcr.at[half], r_pc + half)
        for n, yy in enumerate((yf, yr, yl)):
            pys[half, n] = (po[half, yy] + pcr[half, yy].astype(F32)).astype(BF)
            copies.make(pys.at[half, n], pyr.at[half, n], s_py, r_py + half, p.at(y=yy)).start()

    def keys_of(half):
        total = po[half, y] + pcr[half, y].astype(F32)
        copies.got(pyr.at[half], r_py + half)
        for n in range(3):
            total = total + pyr[half, n].astype(F32)
        for n in range(2):
            kb[2 * half + n, x, 0] = rope(total[:, n * HD : (n + 1) * HD], cosine, sine, 1.0).astype(BF)

    gv.pass_on(1)
    gv.pass_on(2)
    keys_of(0)
    gk.start(0)
    keys_of(1)
    gk.start(1)
    gv.pass_on(3)

    position = zh * 4 + x
    own_docs = jnp.broadcast_to(docs[:, pl.ds(place, rows)], (rows, rows)).T
    row = lax.broadcasted_iota(jnp.int32, (rows, rows), 0)
    col = lax.broadcasted_iota(jnp.int32, (rows, rows), 1)
    for n in range(9):
        block = position - 8 + n
        start = pl.multiple_of(jnp.maximum(block, 0) * rows, rows)
        seen = own_docs == docs[:, pl.ds(start, rows)]
        if n == 8:
            seen = seen & (col <= row)
        column = jnp.where(seen, jnp.where(block >= 0, 0.0, -1e30), -1e30)
        bias[:rows, n * rows : (n + 1) * rows] = column
        bias[rows:, n * rows : (n + 1) * rows] = column
    gk.pass_on(0)
    gk.start(2)
    gk.pass_on(1)
    gk.start(3)
    hat[...] = ha[...].reshape(1024, 768).T
    local_q.wait()
    local_do.wait()

    sk = Scatter(p, copies, dkb, krn, krz, kzs, kacc)
    sv = Scatter(p, copies, dvb, vrn, vrz, vzs, vacc)
    s_ky, r_ky = copies.new_send(), copies.new_recv(KVH)
    s_kp, r_kp = copies.new_send(), copies.new_recv(KVH)

    def key_grad(g):
        cos1, sin1 = spread(tab[...])
        kga[g, j] = rope(sk.end(g), cos1, sin1, -1.0).astype(BF)
        ref = kga.at[g, j]
        for yy in (yf, yr, yl):
            copies.make(ref, ref, s_ky, r_ky + g, p.at(y=yy)).start()
        copies.make(ref, ref, s_kp, r_kp + g, mate).start()

    def key_pass(g):
        copies.got(kga.at[g, 0:3], r_ky + g)
        for yy in (yf, yr, yl):
            ref = kga.at[g, 2 * yy + c]
            copies.make(ref, ref, s_kp, r_kp + g, mate).start()

    nt = (((1,), (1,)), ((), ()))
    tn = (((0,), (0,)), ((), ()))

    u = (x - 2 * c + 4) % 4
    s_x, r_x = copies.new_send(), copies.new_recv(KVH)
    s_z, r_z = copies.new_send(), copies.new_recv(KVH)
    s_l, r_l = copies.new_send(), copies.new_recv(KVH)
    s_y, r_y = copies.new_send(), copies.new_recv(KVH)
    s_c, r_c = copies.new_send(), copies.new_recv(KVH)
    steps = jnp.where(upward, 2 * r + lo - 1, 2 * (4 - r) - lo)
    top = p.at(lo=jnp.where(upward, 1, 0), zh=y)

    def weight_grad(g):
        copies.got(kga.at[g, 0:4], r_kp + g)
        for t in range(2):
            wg[g, t] = jnp.dot(
                hat[t * 384 : (t + 1) * 384, :], kga[g].reshape(1024, HD), preferred_element_type=F32
            ).astype(BF)

            @pl.when(u != t)
            def _():
                d = (u - t + 3) % 4
                copies.make(wg.at[g, t], wxr.at[g, d], s_x, r_x + g, p.at(x=2 * c + t)).start()

    def x_sum(g):
        @pl.when(part)
        def _():
            total = wg[g, b].astype(F32)
            copies.got(wxr.at[g], r_x + g)
            for d in range(3):
                total = total + wxr[g, d].astype(F32)
            wsum[g] = total.astype(BF)

            @pl.when(jnp.logical_not(root))
            def _():
                copies.make(wsum.at[g], wzr.at[g, steps - 1], s_z, r_z + g, top).start()

    def z_sum(g):
        @pl.when(part & root)
        def _():
            total = wsum[g].astype(F32)
            copies.got(wzr.at[g], r_z + g)
            for d in range(3):
                total = total + wzr[g, d].astype(F32)
            wlo[g] = total.astype(BF)
            copies.make(wlo.at[g], wlr.at[g], s_l, r_l + g, p.at(lo=1 - lo)).start()

    def finish(g):
        @pl.when(part & root)
        def _():
            copies.got(wlr.at[g], r_l + g)
            total = wlo[g].astype(F32) + wlr[g].astype(F32)
            wfin[g] = (total * (1.0 / 16.0)).astype(BF)
            for yy in (yf, yr, yl):
                copies.make(wfin.at[g], wfin.at[g], s_y, r_y + g, p.at(y=yy)).start()
            copies.make(wfin.at[g], wfin.at[g], s_c, r_c + g, mate).start()

    def take(g):
        @pl.when(part & jnp.logical_not(root))
        def _():
            copies.got(wfin.at[g], r_y + g)
            copies.make(wfin.at[g], wfin.at[g], s_c, r_c + g, mate).start()

    def keep(g):
        @pl.when(jnp.logical_not(part))
        def _():
            copies.got(wfin.at[g], r_c + g)

        gw_o[:, g * HD : (g + 1) * HD] = wfin[g].astype(F32)

    def value_out(g):
        gv_o[:, g * HD : (g + 1) * HD] = sv.end(g).astype(BF)

    def ready(g):
        gk.end(g)
        gv.end(g)

    def away_copy(n, g):
        at = pl.ds(pl.multiple_of(g * (GROUP * HD), HD), GROUP * HD)
        src, dst = ((out, out_o), (dq, dq_o))[n]
        return pltpu.make_async_copy(src.at[:, at], dst.at[:, at], loc.at[9 + KVH * n + g])

    def head(g, carry):
        ready(g)
        for n in range(9):
            xx, kk = (x + n) % 4, 2 - (x + n) // 4
            kc[n * rows : (n + 1) * rows] = kb[g, xx, kk]
            vc[n * rows : (n + 1) * rows] = vb[g, xx, kk]

        def lanes(h):
            return pl.ds(pl.multiple_of(g * (GROUP * HD) + h * HD, HD), HD)

        for h in range(GROUP):
            qs[h * rows : (h + 1) * rows] = q[:, lanes(h)]
            dos[h * rows : (h + 1) * rows] = do[:, lanes(h)]
        for pair in range(GROUP // 2):
            to = slice(pair * 2 * rows, (pair + 1) * 2 * rows)
            s = lax.dot_general(qs[to], kc[...], nt, preferred_element_type=F32)
            wt = jnp.exp2(s * (scale * math.log2(math.e)) + bias[...])
            inverse = 1.0 / jnp.sum(wt, axis=1, keepdims=True)
            mixed = jnp.dot(wt.astype(BF), vc[...], preferred_element_type=F32)
            attended = (mixed * inverse).astype(BF)
            delta = jnp.sum(dos[to].astype(F32) * attended.astype(F32), axis=1, keepdims=True)
            prob = wt * inverse
            probs[to] = prob.astype(BF)
            dprob = lax.dot_general(dos[to], vc[...], nt, preferred_element_type=F32)
            ds = (prob * (dprob - delta)).astype(BF)
            ds_all[to] = ds
            dquery = (jnp.dot(ds, kc[...], preferred_element_type=F32) * scale).astype(BF)
            for n in range(2):
                out[:, lanes(2 * pair + n)] = attended[n * rows : (n + 1) * rows]
                dq[:, lanes(2 * pair + n)] = dquery[n * rows : (n + 1) * rows]
            if pair == 0:
                @pl.when(g == 0)
                def _():
                    gk.pass_on(2)

                @pl.when(g >= 2)
                def _():
                    sv.across(g - 2)

                @pl.when(g >= 3)
                def _():
                    weight_grad(g - 3)
            if pair == 1:
                @pl.when(g == 0)
                def _():
                    gk.pass_on(3)

                @pl.when(g >= 2)
                def _():
                    key_grad(g - 2)

                @pl.when(g >= 1)
                def _():
                    sk.across(g - 1)
        dkc = (lax.dot_general(ds_all[...], qs[...], tn, preferred_element_type=F32) * scale).astype(BF)
        for n in range(9):
            dkb[g, (x + n) % 4, 2 - (x + n) // 4] = dkc[n * rows : (n + 1) * rows]
        sk.start(g)
        dvc = lax.dot_general(probs[...], dos[...], tn, preferred_element_type=F32).astype(BF)
        for n in range(9):
            dvb[g, (x + n) % 4, 2 - (x + n) // 4] = dvc[n * rows : (n + 1) * rows]
        @pl.when(g < KVH - 1)
        def _():
            sv.start(g)

        away_copy(0, g).start()
        away_copy(1, g).start()

        @pl.when(g >= 2)
        def _():
            key_pass(g - 2)

        return carry

    lax.fori_loop(0, KVH, head, 0)

    x_sum(0)
    weight_grad(1)
    key_grad(2)
    sk.across(3)
    key_pass(2)
    x_sum(1)
    key_grad(3)
    sv.start(3)
    sv.across(2)
    weight_grad(2)
    key_pass(3)
    x_sum(2)
    z_sum(0)
    finish(0)
    weight_grad(3)
    sv.across(3)
    z_sum(1)
    finish(1)
    take(0)
    x_sum(3)
    z_sum(2)
    finish(2)
    take(1)
    keep(0)
    z_sum(3)
    take(2)
    finish(3)
    keep(1)
    keep(2)
    for g in range(KVH):
        value_out(g)
    take(3)
    keep(3)

    copies.sent(seven, s_dir)
    copies.sent(pcs, s_pc)
    copies.sent(pys, s_py)
    for each in (gv, gk, sk, sv):
        each.sends()
    copies.sent(kga.at[:, 0:3], s_ky)
    copies.sent(kga.at[:, 0:4], s_kp)

    @pl.when(forward)
    def _():
        for n in range(NQ):
            @pl.when(jnp.logical_not(root) | (n >= NQ - 2))
            def _():
                copies.sent(wpart(n), s_wz + n)

    @pl.when(part)
    def _():
        copies.sent(wzr, s_wx)
        copies.sent(wsum, s_x)
        copies.sent(wfin, s_c)

        @pl.when(root)
        def _():
            copies.sent(wlo, s_l)
            copies.sent(wzr, s_y)

        @pl.when(jnp.logical_not(root))
        def _():
            copies.sent(wsum, s_z)

    @pl.when(jnp.logical_not(part))
    def _():
        copies.sent(wg, s_x)

    for g in range(KVH):
        away_copy(0, g).wait()
        away_copy(1, g).wait()


def rotation_table(tokens):
    freqs = ROPE_BASE ** (-np.arange(HD // 2) * 2.0 / HD)
    angles = np.arange(tokens)[:, None] * freqs[None, :]
    return np.concatenate([np.cos(angles), np.sin(angles)], axis=1).astype(np.float32)


def place_kernel(a, b, c, d, ao, bo, co, do, av, bv, cv, dv, came, went):
    names = ((a, av, ao), (b, bv, bo), (c, cv, co), (d, dv, do))
    first = [pltpu.make_async_copy(src, mid, came.at[n]) for n, (src, mid, dst) in enumerate(names)]
    second = [pltpu.make_async_copy(mid, dst, went.at[n]) for n, (src, mid, dst) in enumerate(names)]
    for cp in first:
        cp.start()
    for one, two in zip(first, second):
        one.wait()
        two.start()
    for cp in second:
        cp.wait()


def local(inputs, queries, values, key_weight, doc_ids, grad_out):
    rows = HD
    width = KVH * HD
    keys = 9 * rows
    table = jnp.asarray(rotation_table(doc_ids.shape[1]))
    vmem = pl.BlockSpec(memory_space=pltpu.VMEM)
    anywhere = pl.BlockSpec(memory_space=pl.ANY)
    dma = pltpu.SemaphoreType.DMA
    V = pltpu.VMEM
    tile = (rows, HD)
    attn, dq, grad_values, weight_grad = pl.pallas_call(
        whole_kernel,
        out_shape=(
            jax.ShapeDtypeStruct((rows, QH * HD), BF),
            jax.ShapeDtypeStruct((rows, QH * HD), BF),
            jax.ShapeDtypeStruct((rows, width), BF),
            jax.ShapeDtypeStruct((384, width), F32),
        ),
        in_specs=[anywhere, anywhere, anywhere, anywhere, anywhere, vmem, anywhere],
        out_specs=(anywhere, anywhere, vmem, vmem),
        scratch_shapes=[
            V((rows, QH * HD), BF),
            V((rows, QH * HD), BF),
            V((rows, QH * HD), BF),
            V((rows, QH * HD), BF),
            V((4, 2, rows, 768), BF),
            V((768, 1024), BF),
            V((2, 384, width), BF),
            V((KVH, 4, 3) + tile, BF),
            V((KVH, 4, 3) + tile, BF),
            V((2, 4, rows, 256), F32),
            V((2, 4, rows, 256), BF),
            V((2, 4, rows, 256), BF),
            V((2, 3, rows, 256), BF),
            V((2, 3, rows, 256), BF),
            V(tile, F32),
            V((GROUP * rows, keys), BF),
            V((GROUP * rows, keys), BF),
            V((2 * rows, keys), F32),
            V((keys, HD), BF),
            V((keys, HD), BF),
            V((GROUP * rows, HD), BF),
            V((GROUP * rows, HD), BF),
            V((KVH, 4, 3) + tile, BF),
            V((KVH, 4, 3) + tile, BF),
            V((KVH, 6) + tile, BF),
            V((KVH, 6) + tile, BF),
            V((KVH, 2) + tile, BF),
            V((KVH, 2) + tile, BF),
            V((KVH, 2) + tile, BF),
            V((KVH, 2) + tile, BF),
            V((KVH, 3) + tile, F32),
            V((KVH, 3) + tile, F32),
            V((KVH, 8) + tile, BF),
            V((KVH, 2, 384, HD), BF),
            V((KVH, 3, 384, HD), BF),
            V((KVH, 384, HD), BF),
            V((KVH, 3, 384, HD), BF),
            V((KVH, 384, HD), BF),
            V((KVH, 384, HD), BF),
            V((KVH, 384, HD), BF),
            dma((SENDS,)),
            dma((RECVS,)),
            dma((17,)),
        ],
        compiler_params=pltpu.CompilerParams(
            collective_id=0, has_side_effects=True, vmem_limit_bytes=VMEM_LIMIT
        ),
        name="whole",
    )(inputs[0], key_weight, values[0], queries[0], grad_out[0], doc_ids, table)
    attn, dq, grad_values, weight_grad = pl.pallas_call(
        place_kernel,
        out_shape=(
            jax.ShapeDtypeStruct((rows, QH * HD), BF),
            jax.ShapeDtypeStruct((rows, QH * HD), BF),
            jax.ShapeDtypeStruct((rows, width), BF),
            jax.ShapeDtypeStruct((384, width), F32),
        ),
        in_specs=[anywhere] * 4,
        out_specs=(anywhere,) * 4,
        scratch_shapes=[
            V((rows, QH * HD), BF),
            V((rows, QH * HD), BF),
            V((rows, width), BF),
            V((384, width), F32),
            dma((4,)),
            dma((4,)),
        ],
        name="place_results",
    )(attn, dq, grad_values, weight_grad)
    return attn[None], dq[None], grad_values[None], weight_grad


def solution(mesh):
    in_specs = (
        P("dp", "seq", None),
        P("dp", "seq", None),
        P("dp", "seq", None),
        P("seq", None),
        P("dp", None),
        P("dp", "seq", None),
    )
    out_specs = (P("dp", "seq", None), P("dp", "seq", None), P("dp", "seq", None), P("seq", None))
    return jax.shard_map(local, mesh=mesh, in_specs=in_specs, out_specs=out_specs, check_vma=False)
```

time: 785 us -> 129 us (0.16)
  waiting for transfers between devices: 588 us -> 0 us
  Pallas kernels: 0 us -> 128 us
  local copies, waits for them, and re-layouts: 94.3 us -> 0 us
  matrix products: 61.3 us -> 0 us
  other arithmetic: 19.4 us -> 0 us
  between operations: 14.3 us -> 0.64 us
    reduce_scatter x2 -> x0, waiting for transfers between devices: 278 us -> none  [the longest x1 159 us: local(): lax.psum_scatter(lax.dot_general(hidden, key_grad_raw, (((0,), (0,)), (()...]
    all_gather x3 -> x0, waiting for transfers between devices: 195 us -> none  [the longest x1 101 us: local(): lax.all_gather(key_weight, 'seq', axis=0, tiled=True)]
    pallas_call x0 -> x2, Pallas kernels: none -> 128 us  [the longest x1 125 us: local(): pl.pallas_call(whole_kernel, out_shape=(jax.ShapeDtypeStruct((rows, QH *...]
    psum x1 -> x0, waiting for transfers between devices: 114 us -> none  [local(): weight_grad = lax.psum(partial_grad, 'dp') / lax.axis_size('dp')]
    dot_general x30 -> x0, matrix products: 61.3 us -> none  [the longest x8 22.3 us: exp_weights(): jnp.einsum('tkgd,ckd->kgtc', query_heads, key_tile, preferred_element_typ...]
    dynamic_slice x29 -> x0, local copies, waits for them, and re-layouts: 26.4 us -> none  [the longest x28 26.4 us: local(): lax.scan(forward_step, (zero_sum, zero_mix), (key_tiles, value_tiles, doc...]
    dynamic_update_slice x8 -> x0, local copies, waits for them, and re-layouts: 24.4 us -> none  [local(): lax.scan(backward_step, zero_mix, (key_tiles, value_tiles, doc_tiles, anc...]
    unnamed x18 -> x0, local copies, waits for them, and re-layouts: 16.5 us -> none
  transfers between devices with their start and end apart: 6 -> 0, of which waited for: 6 -> 0; matrix products, arithmetic and copies ran while one was open for 4% -> 0% of each run, Pallas kernels for 0% -> 0%
where the time goes in v2:
time: 129 us
  Pallas kernels  128 us (99%)
    pallas_call x1, Pallas kernels, local(): pl.pallas_call(whole_kernel, out_shape=(jax.ShapeDtypeStruct((rows, QH *...  125 us
    pallas_call x1, Pallas kernels, local(): pl.pallas_call(place_kernel, out_shape=(jax.ShapeDtypeStruct((rows, QH *...  2.64 us

profile of v2, /device:TPU:9, one launch (start us, length us, event | category | flops | bytes accessed | tf_op | source)
XLA Modules:
  0.0 128.5 jit_solution(7204863183025648936)
XLA Ops:
  0.6 125.2 %whole.1 = (bf16[128,3072]{1,0:T(8,128)(2,1)}, bf16[128,3072]{1,0:T(8,128)(2,1)}, bf16[128,512]{1,0:T(8,128)(2,1)}, f32[384,512]{1,0:T(8,128)}) custom-call(bf16[128,6144]{1,0:T(8,128)(2,1)} %bitcast.7, bf16[384,512]{1,0:T(8,128)(2,1)} %w.1, bf16[128,512]{1,0:T(8,128)(2,1)} %bitcast.10, bf16[128,3072]{1,0:T(8,128)(2,1)} %bitcast.8, ...), custom_call_target="tpu_custom_call" | custom-call | tf_op jit(solution)/shard_map/whole/pallas_call | solution.py:642
  125.9 2.6 %place_results.1 = (bf16[128,3072]{1,0:T(8,128)(2,1)}, bf16[128,3072]{1,0:T(8,128)(2,1)}, bf16[128,512]{1,0:T(8,128)(2,1)}, f32[384,512]{1,0:T(8,128)}) custom-call(bf16[128,3072]{1,0:T(8,128)(2,1)} %get-tuple-element.12.a, bf16[128,3072]{1,0:T(8,128)(2,1)} %get-tuple-element.13.b, bf16[128,512]{1,0:T(8,128)(2,1)} %get-tuple-element.14.c, ...), custom_call_target="tpu_custom_call" | custom-call | tf_op jit(solution)/shard_map/place_results/pallas_call | solution.py:702

commit v3 on v2

--- a/solution.py
+++ b/solution.py
@@ -17,8 +17,8 @@
 BF = jnp.bfloat16
 F32 = jnp.float32
 NQ = 4
-SENDS = 21
-RECVS = 78
+SENDS = 20
+RECVS = 70
 VMEM_LIMIT = 56 * 1024 * 1024
 
 
@@ -271,8 +271,15 @@
 
     seven = hat.at[0:672]
     s_dir, r_dir = copies.new_send(), copies.new_recv()
-    for yy, cc in ((yf, c), (yf, 1 - c), (yr, c), (yr, 1 - c), (yl, c), (yl, 1 - c), (y, 1 - c)):
+    group = ((yf, c), (yf, 1 - c), (yr, c), (yr, 1 - c), (yl, c), (yl, 1 - c), (y, 1 - c))
+    for yy, cc in group:
         copies.make(piece(yy, cc), ha.at[y, c], s_dir, r_dir, p.at(y=yy, c=cc)).start()
+
+    gv = Gather(p, copies, vb)
+    gk = Gather(p, copies, kb)
+    for cp in local_v:
+        cp.wait()
+    gv.start(0)
 
     @pl.when(part & root)
     def _():
@@ -280,19 +287,12 @@
             copies.sent(wpart(n - 2), s_wz + n - 2)
             w_start(n)
 
-    gv = Gather(p, copies, vb)
-    gk = Gather(p, copies, kb)
-
     @pl.when(takes)
     def _():
         for n in range(NQ):
             copies.got(wpart(n), r_wz + n)
             w_start(n)
 
-    for cp in local_v:
-        cp.wait()
-    gv.start(0)
-
     @pl.when(part)
     def _():
         copies.got(wb.at[0], r_wx)
@@ -302,8 +302,6 @@
         copies.got(wb, r_wx)
 
     gv.start(1)
-    gv.start(2)
-    gv.start(3)
     gv.pass_on(0)
     local_h.wait()
     local_t.wait()
@@ -331,13 +329,14 @@
         for n in range(2):
             kb[2 * half + n, x, 0] = rope(total[:, n * HD : (n + 1) * HD], cosine, sine, 1.0).astype(BF)
 
+    gv.start(2)
+    gv.start(3)
     gv.pass_on(1)
-    gv.pass_on(2)
     keys_of(0)
     gk.start(0)
     keys_of(1)
     gk.start(1)
-    gv.pass_on(3)
+    gv.pass_on(2)
 
     position = zh * 4 + x
     own_docs = jnp.broadcast_to(docs[:, pl.ds(place, rows)], (rows, rows)).T
@@ -356,6 +355,7 @@
     gk.start(2)
     gk.pass_on(1)
     gk.start(3)
+    gv.pass_on(3)
     hat[...] = ha[...].reshape(1024, 768).T
     local_q.wait()
     local_do.wait()
@@ -363,21 +363,13 @@
     sk = Scatter(p, copies, dkb, krn, krz, kzs, kacc)
     sv = Scatter(p, copies, dvb, vrn, vrz, vzs, vacc)
     s_ky, r_ky = copies.new_send(), copies.new_recv(KVH)
-    s_kp, r_kp = copies.new_send(), copies.new_recv(KVH)
 
     def key_grad(g):
         cos1, sin1 = spread(tab[...])
         kga[g, j] = rope(sk.end(g), cos1, sin1, -1.0).astype(BF)
         ref = kga.at[g, j]
-        for yy in (yf, yr, yl):
-            copies.make(ref, ref, s_ky, r_ky + g, p.at(y=yy)).start()
-        copies.make(ref, ref, s_kp, r_kp + g, mate).start()
-
-    def key_pass(g):
-        copies.got(kga.at[g, 0:3], r_ky + g)
-        for yy in (yf, yr, yl):
-            ref = kga.at[g, 2 * yy + c]
-            copies.make(ref, ref, s_kp, r_kp + g, mate).start()
+        for yy, cc in group:
+            copies.make(ref, ref, s_ky, r_ky + g, p.at(y=yy, c=cc)).start()
 
     nt = (((1,), (1,)), ((), ()))
     tn = (((0,), (0,)), ((), ()))
@@ -386,13 +378,13 @@
     s_x, r_x = copies.new_send(), copies.new_recv(KVH)
     s_z, r_z = copies.new_send(), copies.new_recv(KVH)
     s_l, r_l = copies.new_send(), copies.new_recv(KVH)
+    s_c = copies.new_send()
     s_y, r_y = copies.new_send(), copies.new_recv(KVH)
-    s_c, r_c = copies.new_send(), copies.new_recv(KVH)
     steps = jnp.where(upward, 2 * r + lo - 1, 2 * (4 - r) - lo)
     top = p.at(lo=jnp.where(upward, 1, 0), zh=y)
 
     def weight_grad(g):
-        copies.got(kga.at[g, 0:4], r_kp + g)
+        copies.got(kga.at[g, 0:7], r_ky + g)
         for t in range(2):
             wg[g, t] = jnp.dot(
                 hat[t * 384 : (t + 1) * 384, :], kga[g].reshape(1024, HD), preferred_element_type=F32
@@ -434,18 +426,18 @@
             wfin[g] = (total * (1.0 / 16.0)).astype(BF)
             for yy in (yf, yr, yl):
                 copies.make(wfin.at[g], wfin.at[g], s_y, r_y + g, p.at(y=yy)).start()
-            copies.make(wfin.at[g], wfin.at[g], s_c, r_c + g, mate).start()
+            copies.make(wfin.at[g], wfin.at[g], s_c, r_y + g, mate).start()
 
     def take(g):
         @pl.when(part & jnp.logical_not(root))
         def _():
             copies.got(wfin.at[g], r_y + g)
-            copies.make(wfin.at[g], wfin.at[g], s_c, r_c + g, mate).start()
+            copies.make(wfin.at[g], wfin.at[g], s_c, r_y + g, mate).start()
 
     def keep(g):
         @pl.when(jnp.logical_not(part))
         def _():
-            copies.got(wfin.at[g], r_c + g)
+            copies.got(wfin.at[g], r_y + g)
 
         gw_o[:, g * HD : (g + 1) * HD] = wfin[g].astype(F32)
 
@@ -496,79 +488,75 @@
                 def _():
                     gk.pass_on(2)
 
+                @pl.when(g == 2)
+                def _():
+                    sk.across(0)
+
                 @pl.when(g >= 2)
                 def _():
                     sv.across(g - 2)
-
-                @pl.when(g >= 3)
-                def _():
-                    weight_grad(g - 3)
             if pair == 1:
                 @pl.when(g == 0)
                 def _():
                     gk.pass_on(3)
 
-                @pl.when(g >= 2)
-                def _():
-                    key_grad(g - 2)
-
-                @pl.when(g >= 1)
-                def _():
-                    sk.across(g - 1)
-        dkc = (lax.dot_general(ds_all[...], qs[...], tn, preferred_element_type=F32) * scale).astype(BF)
+        dkc = (lax.dot_general(qs[...], ds_all[...], tn, preferred_element_type=F32) * scale).astype(BF)
+        @pl.when(g >= 2)
+        def _():
+            sk.across(g - 1)
+
         for n in range(9):
-            dkb[g, (x + n) % 4, 2 - (x + n) // 4] = dkc[n * rows : (n + 1) * rows]
+            dkb[g, (x + n) % 4, 2 - (x + n) // 4] = dkc[:, n * rows : (n + 1) * rows].T
         sk.start(g)
-        dvc = lax.dot_general(probs[...], dos[...], tn, preferred_element_type=F32).astype(BF)
+
+        @pl.when(g >= 2)
+        def _():
+            key_grad(g - 2)
+
+        dvc = lax.dot_general(dos[...], probs[...], tn, preferred_element_type=F32).astype(BF)
         for n in range(9):
-            dvb[g, (x + n) % 4, 2 - (x + n) // 4] = dvc[n * rows : (n + 1) * rows]
+            dvb[g, (x + n) % 4, 2 - (x + n) // 4] = dvc[:, n * rows : (n + 1) * rows].T
         @pl.when(g < KVH - 1)
         def _():
             sv.start(g)
 
         away_copy(0, g).start()
         away_copy(1, g).start()
-
-        @pl.when(g >= 2)
-        def _():
-            key_pass(g - 2)
-
         return carry
 
     lax.fori_loop(0, KVH, head, 0)
 
+    weight_grad(0)
+    sk.across(3)
+    key_grad(2)
+    weight_grad(1)
     x_sum(0)
-    weight_grad(1)
-    key_grad(2)
-    sk.across(3)
-    key_pass(2)
+    sv.across(2)
+    key_grad(3)
     x_sum(1)
-    key_grad(3)
+    weight_grad(2)
+    z_sum(0)
+    weight_grad(3)
     sv.start(3)
-    sv.across(2)
-    weight_grad(2)
-    key_pass(3)
+    finish(0)
     x_sum(2)
-    z_sum(0)
-    finish(0)
-    weight_grad(3)
+    z_sum(1)
+    x_sum(3)
+    finish(1)
+    z_sum(2)
+    take(0)
+    finish(2)
+    z_sum(3)
+    take(1)
+    finish(3)
+    take(2)
     sv.across(3)
-    z_sum(1)
-    finish(1)
-    take(0)
-    x_sum(3)
-    z_sum(2)
-    finish(2)
-    take(1)
     keep(0)
-    z_sum(3)
-    take(2)
-    finish(3)
     keep(1)
     keep(2)
+    take(3)
     for g in range(KVH):
         value_out(g)
-    take(3)
     keep(3)
 
     copies.sent(seven, s_dir)
@@ -576,8 +564,7 @@
     copies.sent(pys, s_py)
     for each in (gv, gk, sk, sv):
         each.sends()
-    copies.sent(kga.at[:, 0:3], s_ky)
-    copies.sent(kga.at[:, 0:4], s_kp)
+    copies.sent(kga.at[:, 0:7], s_ky)
 
     @pl.when(forward)
     def _():
@@ -589,7 +576,7 @@
     @pl.when(part)
     def _():
         copies.sent(wzr, s_wx)
-        copies.sent(wsum, s_x)
+        copies.sent(wfin, s_x)
         copies.sent(wfin, s_c)
 
         @pl.when(root)

time: 129 us -> 124 us (0.961); the launches traced: 129 us -> 122 us
  Pallas kernels: 128 us -> 121 us
    pallas_call x1, Pallas kernels: 125 us -> 119 us  [local(): pl.pallas_call(whole_kernel, out_shape=(jax.ShapeDtypeStruct((rows, QH *...]
where the time goes in v3:
time: 124 us; the launch traced here: 122 us
  Pallas kernels  121 us (98%)
    pallas_call x1, Pallas kernels, local(): pl.pallas_call(whole_kernel, out_shape=(jax.ShapeDtypeStruct((rows, QH *...  119 us
    pallas_call x1, Pallas kernels, local(): pl.pallas_call(place_kernel, out_shape=(jax.ShapeDtypeStruct((rows, QH *...  2.64 us

profile of v3, /device:TPU:9, one launch (start us, length us, event | category | flops | bytes accessed | tf_op | source)
XLA Modules:
  0.0 122.0 jit_solution(3407195551820543813)
XLA Ops:
  0.6 118.7 %whole.1 = (bf16[128,3072]{1,0:T(8,128)(2,1)}, bf16[128,3072]{1,0:T(8,128)(2,1)}, bf16[128,512]{1,0:T(8,128)(2,1)}, f32[384,512]{1,0:T(8,128)}) custom-call(bf16[128,6144]{1,0:T(8,128)(2,1)} %bitcast.7, bf16[384,512]{1,0:T(8,128)(2,1)} %w.1, bf16[128,512]{1,0:T(8,128)(2,1)} %bitcast.10, bf16[128,3072]{1,0:T(8,128)(2,1)} %bitcast.8, ...), custom_call_target="tpu_custom_call" | custom-call | tf_op jit(solution)/shard_map/whole/pallas_call | solution.py:629
  119.3 2.6 %place_results.1 = (bf16[128,3072]{1,0:T(8,128)(2,1)}, bf16[128,3072]{1,0:T(8,128)(2,1)}, bf16[128,512]{1,0:T(8,128)(2,1)}, f32[384,512]{1,0:T(8,128)}) custom-call(bf16[128,3072]{1,0:T(8,128)(2,1)} %get-tuple-element.12.a, bf16[128,3072]{1,0:T(8,128)(2,1)} %get-tuple-element.13.b, bf16[128,512]{1,0:T(8,128)(2,1)} %get-tuple-element.14.c, ...), custom_call_target="tpu_custom_call" | custom-call | tf_op jit(solution)/shard_map/place_results/pallas_call | solution.py:689

commit v4 on v3

--- a/solution.py
+++ b/solution.py
@@ -16,9 +16,9 @@
 MESH = pl.DeviceIdType.MESH
 BF = jnp.bfloat16
 F32 = jnp.float32
-NQ = 4
-SENDS = 20
-RECVS = 70
+NQ = 8
+SENDS = 24
+RECVS = 74
 VMEM_LIMIT = 56 * 1024 * 1024
 
 

time: 124 us -> 122 us (0.984); the launches traced: 122 us -> 122 us
  no operation moved by 1% of the time
where the time goes in v4:
time: 122 us
  Pallas kernels  121 us (99%)
    pallas_call x1, Pallas kernels, local(): pl.pallas_call(whole_kernel, out_shape=(jax.ShapeDtypeStruct((rows, QH *...  119 us
    pallas_call x1, Pallas kernels, local(): pl.pallas_call(place_kernel, out_shape=(jax.ShapeDtypeStruct((rows, QH *...  2.64 us

profile of v4, /device:TPU:9, one launch (start us, length us, event | category | flops | bytes accessed | tf_op | source)
XLA Modules:
  0.0 122.1 jit_solution(4691236864069784098)
XLA Ops:
  0.6 118.9 %whole.1 = (bf16[128,3072]{1,0:T(8,128)(2,1)}, bf16[128,3072]{1,0:T(8,128)(2,1)}, bf16[128,512]{1,0:T(8,128)(2,1)}, f32[384,512]{1,0:T(8,128)}) custom-call(bf16[128,6144]{1,0:T(8,128)(2,1)} %bitcast.7, bf16[384,512]{1,0:T(8,128)(2,1)} %w.1, bf16[128,512]{1,0:T(8,128)(2,1)} %bitcast.10, bf16[128,3072]{1,0:T(8,128)(2,1)} %bitcast.8, ...), custom_call_target="tpu_custom_call" | custom-call | tf_op jit(solution)/shard_map/whole/pallas_call | solution.py:629
  119.5 2.6 %place_results.1 = (bf16[128,3072]{1,0:T(8,128)(2,1)}, bf16[128,3072]{1,0:T(8,128)(2,1)}, bf16[128,512]{1,0:T(8,128)(2,1)}, f32[384,512]{1,0:T(8,128)}) custom-call(bf16[128,3072]{1,0:T(8,128)(2,1)} %get-tuple-element.12.a, bf16[128,3072]{1,0:T(8,128)(2,1)} %get-tuple-element.13.b, bf16[128,512]{1,0:T(8,128)(2,1)} %get-tuple-element.14.c, ...), custom_call_target="tpu_custom_call" | custom-call | tf_op jit(solution)/shard_map/place_results/pallas_call | solution.py:689

commit v5 on v4

--- a/solution.py
+++ b/solution.py
@@ -604,7 +604,13 @@
 
 
 def place_kernel(a, b, c, d, ao, bo, co, do, av, bv, cv, dv, came, went):
-    names = ((a, av, ao), (b, bv, bo), (c, cv, co), (d, dv, do))
+    names = []
+    for n in range(4):
+        cols = pl.ds(n * (QH * HD // 4), QH * HD // 4)
+        names += [tuple(r.at[:, cols] for r in (a, av, ao)), tuple(r.at[:, cols] for r in (b, bv, bo))]
+    for n in range(4):
+        names.append(tuple(r.at[pl.ds(n * 96, 96), :] for r in (d, dv, do)))
+    names.append((c, cv, co))
     first = [pltpu.make_async_copy(src, mid, came.at[n]) for n, (src, mid, dst) in enumerate(names)]
     second = [pltpu.make_async_copy(mid, dst, went.at[n]) for n, (src, mid, dst) in enumerate(names)]
     for cp in first:
@@ -701,8 +707,8 @@
             V((rows, QH * HD), BF),
             V((rows, width), BF),
             V((384, width), F32),
-            dma((4,)),
-            dma((4,)),
+            dma((13,)),
+            dma((13,)),
         ],
         name="place_results",
     )(attn, dq, grad_values, weight_grad)

time: 122 us -> 122 us (level)
  no operation moved by 1% of the time
where the time goes in v5:
time: 122 us
  Pallas kernels  122 us (100%)
    pallas_call x1, Pallas kernels, local(): pl.pallas_call(whole_kernel, out_shape=(jax.ShapeDtypeStruct((rows, QH *...  119 us
    pallas_call x1, Pallas kernels, local(): pl.pallas_call(place_kernel, out_shape=(jax.ShapeDtypeStruct((rows, QH *...  2.69 us

profile of v5, /device:TPU:9, one launch (start us, length us, event | category | flops | bytes accessed | tf_op | source)
XLA Modules:
  0.0 122.2 jit_solution(14865204836112054247)
XLA Ops:
  0.6 118.9 %whole.1 = (bf16[128,3072]{1,0:T(8,128)(2,1)}, bf16[128,3072]{1,0:T(8,128)(2,1)}, bf16[128,512]{1,0:T(8,128)(2,1)}, f32[384,512]{1,0:T(8,128)}) custom-call(bf16[128,6144]{1,0:T(8,128)(2,1)} %bitcast.7, bf16[384,512]{1,0:T(8,128)(2,1)} %w.1, bf16[128,512]{1,0:T(8,128)(2,1)} %bitcast.10, bf16[128,3072]{1,0:T(8,128)(2,1)} %bitcast.8, ...), custom_call_target="tpu_custom_call" | custom-call | tf_op jit(solution)/shard_map/whole/pallas_call | solution.py:635
  119.5 2.7 %place_results.1 = (bf16[128,3072]{1,0:T(8,128)(2,1)}, bf16[128,3072]{1,0:T(8,128)(2,1)}, bf16[128,512]{1,0:T(8,128)(2,1)}, f32[384,512]{1,0:T(8,128)}) custom-call(bf16[128,3072]{1,0:T(8,128)(2,1)} %get-tuple-element.12.a, bf16[128,3072]{1,0:T(8,128)(2,1)} %get-tuple-element.13.b, bf16[128,512]{1,0:T(8,128)(2,1)} %get-tuple-element.14.c, ...), custom_call_target="tpu_custom_call" | custom-call | tf_op jit(solution)/shard_map/place_results/pallas_call | solution.py:695
